TPU v7x, 256 devices: a whole 4x4x8 slice. The times are simulated.
256 devices in a mesh: gx: 32 (over y_hi, z, core), gy: 8 (over y_lo, x).
Axes of the slice: x: 4, y: 4 (y_hi: 2, y_lo: 2; y = y_hi * 2 + y_lo), z: 8, core: 2. Of those that a mesh axis runs over, the one named last changes fastest.
Arguments:
- target: float32 [512, 128, 1024], P('gx', None, 'gy'), may hold values from -6 to 6
- plane_xy: float32 [32, 512, 1024], P(None, 'gx', 'gy'), may hold values from 0.4 to 1.6
- plane_xz: float32 [32, 512, 128], P(None, 'gx', 'gy'), may hold values from 0.4 to 1.6
- plane_yz: float32 [32, 128, 1024], P(None, 'gx', 'gy'), may hold values from 0.4 to 1.6
- first_xy: float32 [32, 512, 1024], P(None, 'gx', 'gy'), may hold values from -6 to 6
- first_xz: float32 [32, 512, 128], P(None, 'gx', 'gy'), may hold values from -6 to 6
- first_yz: float32 [32, 128, 1024], P(None, 'gx', 'gy'), may hold values from -6 to 6
- second_xy: float32 [32, 512, 1024], P(None, 'gx', 'gy'), may hold values from 0.5 to 8
- second_xz: float32 [32, 512, 128], P(None, 'gx', 'gy'), may hold values from 0.5 to 8
- second_yz: float32 [32, 128, 1024], P(None, 'gx', 'gy'), may hold values from 0.5 to 8
- w_hidden: bfloat16 [32, 32], replicated, may hold values from -1 to 1
- b_hidden: float32 [32], replicated, may hold values from -3 to 3
- w_output: bfloat16 [32], replicated, may hold values from -1 to 1
- b_output: float32 [1], replicated, may hold values from -3 to 3
Outputs:
- updated_xy: float32 [32, 512, 1024], P(None, 'gx', 'gy')
- updated_xz: float32 [32, 512, 128], P(None, 'gx', 'gy')
- updated_yz: float32 [32, 128, 1024], P(None, 'gx', 'gy')
- mean_xy: float32 [32, 512, 1024], P(None, 'gx', 'gy')
- mean_xz: float32 [32, 512, 128], P(None, 'gx', 'gy')
- mean_yz: float32 [32, 128, 1024], P(None, 'gx', 'gy')
- square_xy: float32 [32, 512, 1024], P(None, 'gx', 'gy')
- square_xz: float32 [32, 512, 128], P(None, 'gx', 'gy')
- square_yz: float32 [32, 128, 1024], P(None, 'gx', 'gy')
All inputs are finite; a program needn't handle non-finite values.
Results may differ from a plain program's by a relative error of at most 0.00053.
Values sent between devices are 32-bit elements; how exact they have to be, the bound alone decides.
A program may use at most 64 MiB of HBM per device.

v0:
```python
import jax
import jax.numpy as jnp
from jax import lax
from jax.sharding import PartitionSpec as P

STEPS = 2
START = 20


SMOOTHING = 0.5
BETA_ONE = 0.9
BETA_TWO = 0.99
LEARN_RATE = 0.01
EPSILON = 1e-08


def padded_2(x, sides, width):
    for axis, dim in sides:
        peers, length = (lax.axis_size(axis), x.shape[dim])
        up = [(i, (i + 1) % peers) for i in range(peers - 1)]
        down = [(j, i) for i, j in up]
        last = lax.slice_in_dim(x, length - width, length, axis=dim)
        first = lax.slice_in_dim(x, 0, width, axis=dim)
        before = lax.ppermute(last, axis, up)
        after = lax.ppermute(first, axis, down)
        x = jnp.concatenate([before, x, after], axis=dim)
    return x


def smooth(plane):
    padded = padded_2(plane, (("gx", 1), ("gy", 2)), 1)
    down = padded[:, 1:, 1:-1] - padded[:, :-1, 1:-1]
    across = padded[:, 1:-1, 1:] - padded[:, 1:-1, :-1]
    row_count = down.shape[1]
    col_count = across.shape[2]
    row_places = jnp.arange(row_count)
    col_places = jnp.arange(col_count)
    lowest_x = lax.axis_index("gx") == 0
    highest_x = lax.axis_index("gx") == lax.axis_size("gx") - 1
    lowest_y = lax.axis_index("gy") == 0
    highest_y = lax.axis_index("gy") == lax.axis_size("gy") - 1
    row_keeps = jnp.where(
        (row_places == 0) & lowest_x | (row_places == row_count - 1) & highest_x, 0.0, 1.0
    )
    col_keeps = jnp.where(
        (col_places == 0) & lowest_y | (col_places == col_count - 1) & highest_y, 0.0, 1.0
    )
    down = down * row_keeps[None, :, None]
    across = across * col_keeps[None, None, :]
    return (
        2.0 * SMOOTHING * (down[:, :-1, :] - down[:, 1:, :] + across[:, :, :-1] - across[:, :, 1:])
    )


def data_grads(target, plane_xy, whole_xz, whole_yz, w_hidden, b_hidden, w_output, b_output):
    weights_out = w_output.astype(jnp.float32)

    def one_row(running, inputs):
        target_row, row_xy, row_xz = inputs
        cross = row_xz[:, :, None] * whole_yz
        features = (row_xy[:, None, :] * cross).astype(jnp.bfloat16)
        preact = (
            jnp.einsum("ch,czy->hzy", w_hidden, features, preferred_element_type=jnp.float32)
            + b_hidden[:, None, None]
        )
        sigma = jax.nn.sigmoid(preact)
        hidden = (preact * sigma).astype(jnp.bfloat16)
        output = (
            jnp.einsum("h,hzy->zy", w_output, hidden, preferred_element_type=jnp.float32)
            + b_output[0]
        )
        residual = output - target_row
        back_hidden = (
            weights_out[:, None, None] * residual[None] * (sigma * (1.0 + preact * (1.0 - sigma)))
        ).astype(jnp.bfloat16)
        back_feature = jnp.einsum(
            "ch,hzy->czy", w_hidden, back_hidden, preferred_element_type=jnp.float32
        )
        grad_row_xy = jnp.sum(back_feature * cross, axis=1)
        with_xy = back_feature * row_xy[:, None, :]
        grad_row_xz = jnp.sum(with_xy * whole_yz, axis=2)
        running = running + with_xy * row_xz[:, :, None]
        return (running, (grad_row_xy, grad_row_xz))

    start = jnp.zeros(whole_yz.shape, jnp.float32)
    grad_yz, (rows_xy, rows_xz) = lax.scan(
        one_row, start, (target, jnp.moveaxis(plane_xy, 1, 0), jnp.moveaxis(whole_xz, 1, 0))
    )
    return (jnp.moveaxis(rows_xy, 0, 1), jnp.moveaxis(rows_xz, 0, 1), grad_yz)


def adam(plane, first, second, grads, count):
    first = BETA_ONE * first + (1.0 - BETA_ONE) * grads
    second = BETA_TWO * second + (1.0 - BETA_TWO) * grads * grads
    corr_one = 1.0 - BETA_ONE**count
    corr_two = 1.0 - BETA_TWO**count
    plane = plane - LEARN_RATE * (first / corr_one) / (jnp.sqrt(second / corr_two) + EPSILON)
    return (plane, first, second)


def per_device(
    target,
    plane_xy,
    plane_xz,
    plane_yz,
    first_xy,
    first_xz,
    first_yz,
    second_xy,
    second_xz,
    second_yz,
    w_hidden,
    b_hidden,
    w_output,
    b_output,
):
    for iteration in range(STEPS):
        whole_xz = lax.all_gather(plane_xz, "gy", axis=2, tiled=True)
        whole_yz = lax.all_gather(plane_yz, "gx", axis=1, tiled=True)
        grad_xy, term_xz, term_yz = data_grads(
            target, plane_xy, whole_xz, whole_yz, w_hidden, b_hidden, w_output, b_output
        )
        grad_xy = grad_xy + smooth(plane_xy)
        grad_xz = lax.psum_scatter(term_xz, "gy", scatter_dimension=2, tiled=True) + smooth(
            plane_xz
        )
        grad_yz = lax.psum_scatter(term_yz, "gx", scatter_dimension=1, tiled=True) + smooth(
            plane_yz
        )
        count = START + iteration + 1
        plane_xy, first_xy, second_xy = adam(plane_xy, first_xy, second_xy, grad_xy, count)
        plane_xz, first_xz, second_xz = adam(plane_xz, first_xz, second_xz, grad_xz, count)
        plane_yz, first_yz, second_yz = adam(plane_yz, first_yz, second_yz, grad_yz, count)
    return (
        plane_xy,
        plane_xz,
        plane_yz,
        first_xy,
        first_xz,
        first_yz,
        second_xy,
        second_xz,
        second_yz,
    )


def solution(mesh):
    return jax.shard_map(
        per_device,
        mesh=mesh,
        in_specs=(
            P("gx", None, "gy"),
            P(None, "gx", "gy"),
            P(None, "gx", "gy"),
            P(None, "gx", "gy"),
            P(None, "gx", "gy"),
            P(None, "gx", "gy"),
            P(None, "gx", "gy"),
            P(None, "gx", "gy"),
            P(None, "gx", "gy"),
            P(None, "gx", "gy"),
            P(),
            P(),
            P(),
            P(),
        ),
        out_specs=(
            P(None, "gx", "gy"),
            P(None, "gx", "gy"),
            P(None, "gx", "gy"),
            P(None, "gx", "gy"),
            P(None, "gx", "gy"),
            P(None, "gx", "gy"),
            P(None, "gx", "gy"),
            P(None, "gx", "gy"),
            P(None, "gx", "gy"),
        ),
        check_vma=False,
    )
```

profile of v0, /device:TPU:1, one launch (start us, length us, event | category | flops | bytes accessed | tf_op | source)
XLA Modules:
  0.0 943.3 jit_solution(12423835988143817830)
XLA Ops:
  11.2 28.4 %all_gather.12 = f32[32,16,128]{0,2,1:T(8,128)} all-gather(f32[32,16,16]{0,2,1:T(8,128)} %param.20), channel_id=1, replica_groups=mesh['gx'=32,'gy'=8] {'gy'}, dimensions={2}, use_global_device_ids=true | all-gather | bytes 294912 | tf_op jit(solution)/shard_map/all_gather | solution.py:118
  39.6 56.0 %all-gather.3.cloned.1.call-done = f32[32,128,128]{2,0,1:T(8,128)} async-done(((f32[32,4,128]{2,0,1:T(8,128)}), f32[32,128,128]{2,0,1:T(8,128)}) %all-gather.3.cloned.1.call-update) | async-done | bytes 2097168 | tf_op jit(solution)/shard_map/all_gather | solution.py:119
  96.5 218.2 %while.30 = (s32[]{:T(128)}, f32[32,128,128]{2,0,1:T(8,128)}, f32[16,32,128]{2,0,1:T(8,128)}, f32[16,32,128]{1,2,0:T(8,128)S(1)}, f32[32]{0:T(128)S(1)}, /*index...) while((s32[]{:T(128)}, f32[32,128,128]{2,0,1:T(8,128)}, ...), condition=%wide.region_3.4_spmd.clone, body=%wide.region_0.3_spmd.clone.sunk | while | flops 83386368 | bytes 32117412 | solution.py:86
  103.2 4.7 multiply_reduce_fusion.4
  116.2 5.3 multiply_reduce_fusion.4
  129.9 5.3 multiply_reduce_fusion.4
  143.6 5.4 multiply_reduce_fusion.4
  157.2 5.3 multiply_reduce_fusion.4
  170.9 5.3 multiply_reduce_fusion.4
  184.6 5.4 multiply_reduce_fusion.4
  198.3 5.3 multiply_reduce_fusion.4
  211.9 5.3 multiply_reduce_fusion.4
  225.6 5.4 multiply_reduce_fusion.4
  239.3 5.3 multiply_reduce_fusion.4
  253.0 5.3 multiply_reduce_fusion.4
  266.7 5.4 multiply_reduce_fusion.4
  280.3 5.3 multiply_reduce_fusion.4
  294.0 5.3 multiply_reduce_fusion.4
  307.7 5.4 multiply_reduce_fusion.4
  315.6 2.5 collective-permute-start.9
  320.1 3.0 collective-permute-done.8
  324.5 4.0 collective-permute-start.11
  330.2 95.0 %reduce-scatter.7.cloned.1.call-done = f32[32,4,128]{2,0,1:T(8,128)} async-done(((f32[32,128,128]{2,0,1:T(8,128)}), f32[32,4,128]{2,0,1:T(8,128)}) %reduce-scatter.7.cloned.1.call-update) | async-done | bytes 65552 | tf_op jit(solution)/shard_map/reduce_scatter | solution.py:127
  427.0 7.7 collective-permute-start
  436.8 2.4 collective-permute-start.5
  441.2 3.0 collective-permute-done.4
  445.5 4.1 collective-permute-start.7
  452.2 4.3 collective-permute-start.3
  456.6 11.3 %collective-permute-done.2 = f32[32,18,1]{2,1,0:T(8,128)S(1)} collective-permute-done((f32[32,18,1]{2,1,0:T(8,128)S(1)}, f32[32,18,1]{2,1,0:T(8,128)S(1)}, u32[]{:S(2)}, u32[]{:S(2)}) %collective-permute-start.2) | collective-permute-done | bytes 2336 | tf_op jit(solution)/shard_map/ppermute | solution.py:25
  471.8 29.8 %all_gather.14 = f32[32,16,128]{0,2,1:T(8,128)} all-gather(f32[32,16,16]{0,2,1:T(8,128)S(1)} %get-tuple-element.352), channel_id=1, replica_groups=mesh['gx'=32,'gy'=8] {'gy'}, dimensions={2}, use_global_device_ids=true | all-gather | bytes 294912 | tf_op jit(solution)/shard_map/all_gather | solution.py:118
  501.5 56.0 %all-gather.5.cloned.1.call-done = f32[32,128,128]{2,0,1:T(8,128)} async-done(((f32[32,4,128]{2,0,1:T(8,128)}), f32[32,128,128]{2,0,1:T(8,128)}) %all-gather.5.cloned.1.call-update) | async-done | bytes 2097168 | tf_op jit(solution)/shard_map/all_gather | solution.py:119
  559.4 216.8 %while.31 = (s32[]{:T(128)}, f32[32,128,128]{2,0,1:T(8,128)}, f32[16,32,128]{2,0,1:T(8,128)}, f32[16,32,128]{1,2,0:T(8,128)}, f32[32]{0:T(128)S(1)}, /*index=5*/...) while((s32[]{:T(128)}, f32[32,128,128]{2,0,1:T(8,128)}, ...), condition=%wide.region_9.10_spmd.clone, body=%wide.region_6.9_spmd.clone.sunk | while | flops 83386368 | bytes 32068768 | solution.py:86
  560.3 2.2 fusion.108
  565.4 4.7 multiply_reduce_fusion.5
  578.4 5.3 multiply_reduce_fusion.5
  592.0 5.3 multiply_reduce_fusion.5
  605.5 5.3 multiply_reduce_fusion.5
  614.0 2.2 fusion.108
  619.1 5.3 multiply_reduce_fusion.5
  632.7 5.3 multiply_reduce_fusion.5
  646.3 5.3 multiply_reduce_fusion.5
  659.9 5.3 multiply_reduce_fusion.5
  668.3 2.2 fusion.108
  673.5 5.3 multiply_reduce_fusion.5
  687.1 5.3 multiply_reduce_fusion.5
  700.7 5.3 multiply_reduce_fusion.5
  709.1 2.2 fusion.108
  714.3 5.3 multiply_reduce_fusion.5
  722.7 2.2 fusion.108
  727.9 5.3 multiply_reduce_fusion.5
  736.3 2.2 fusion.108
  741.5 5.3 multiply_reduce_fusion.5
  755.0 5.3 multiply_reduce_fusion.5
  763.5 2.2 fusion.108
  768.6 5.3 multiply_reduce_fusion.5
  778.5 3.4 collective-permute-start.13
  784.3 4.1 collective-permute-start.15
  790.5 4.8 collective-permute-start.17
  795.3 5.2 collective-permute-done.14
  800.5 2.7 collective-permute-done.15
  804.8 4.8 collective-permute-start.19
  811.9 3.4 collective-permute-start.21
  817.7 4.0 collective-permute-start.23
  827.2 106.2 %reduce-scatter.11.cloned.1.call-done = f32[32,4,128]{2,0,1:T(8,128)} async-done(((f32[32,128,128]{2,0,1:T(8,128)}), f32[32,4,128]{2,0,1:T(8,128)}) %reduce-scatter.11.cloned.1.call-update) | async-done | bytes 65552 | tf_op jit(solution)/shard_map/reduce_scatter | solution.py:127
  (489 shorter events, 295.3 us)
Async XLA Ops:
  7.2 89.3 %copy-start.24 = (bf16[32]{0:T(256)(128)(2,1)S(1)}, bf16[32]{0:T(256)(128)(2,1)}, u32[]{:S(2)}) copy-start(bf16[32]{0:T(256)(128)(2,1)} %param.30) | copy-start | bytes 196
  7.2 89.3 %copy-start.12 = (bf16[32,32]{1,0:T(8,128)(2,1)S(1)}, bf16[32,32]{1,0:T(8,128)(2,1)}, u32[]{:S(2)}) copy-start(bf16[32,32]{1,0:T(8,128)(2,1)} %param.28) | copy-start | bytes 6148
  7.2 89.3 %copy-start.25 = (f32[32]{0:T(128)S(1)}, f32[32]{0:T(128)}, u32[]{:S(2)}) copy-start(f32[32]{0:T(128)} %param.29) | copy-start | bytes 388
  7.2 88.4 %all-gather.3.cloned.1.call-start = ((), (), s32[]{:S(2)}) async-start(), calls=%async_computation.4 | async-start | bytes 2162688 | tf_op jit(solution)/shard_map/all_gather | solution.py:119
  8.8 416.5 %reduce-scatter.7.cloned.1.call-start = ((), (), s32[]{:S(2)}) async-start(), calls=%async_computation.6 | async-start | bytes 2162688 | tf_op jit(solution)/shard_map/reduce_scatter | solution.py:127
  314.7 13.9 %copy-start.5 = (f32[16,32,128]{1,2,0:T(8,128)}, f32[16,32,128]{1,2,0:T(8,128)S(1)}, u32[]{:S(2)}) copy-start(f32[16,32,128]{1,2,0:T(8,128)S(1)} %get-tuple-element.148) | copy-start | bytes 786436
  314.7 5.4 copy-start.14
  314.7 110.6 %copy-start.20 = (f32[32,4,128]{2,1,0:T(4,128)S(1)}, f32[32,4,128]{2,1,0:T(4,128)}, u32[]{:S(2)}) copy-start(f32[32,4,128]{2,1,0:T(4,128)} %param.24) | copy-start | bytes 196612
  314.7 110.6 %copy-start.21 = (f32[32,4,128]{2,1,0:T(4,128)S(1)}, f32[32,4,128]{2,1,0:T(4,128)}, u32[]{:S(2)}) copy-start(f32[32,4,128]{2,1,0:T(4,128)} %param.27) | copy-start | bytes 196612
  314.7 112.3 %copy-start.4 = (f32[32,16,128]{2,1,0:T(8,128)S(1)}, f32[32,16,128]{2,1,0:T(8,128)}, u32[]{:S(2)}) copy-start(f32[32,16,128]{2,1,0:T(8,128)} %param.19) | copy-start | bytes 786436
  314.7 122.1 %copy-start.7 = (f32[32,16,16]{0,2,1:T(8,128)S(1)}, f32[32,16,16]{0,2,1:T(8,128)}, u32[]{:S(2)}) copy-start(f32[32,16,16]{0,2,1:T(8,128)} %param.20) | copy-start | bytes 98308
  314.7 155.3 %reduce-scatter.5.cloned.1.call-start = ((), (), s32[]{:S(2)}) async-start(), calls=%async_computation.5 | async-start | bytes 1179648 | tf_op jit(solution)/shard_map/reduce_scatter | solution.py:124
  315.6 4.5 collective-permute-start.9
  318.1 5.1 collective-permute-start.8
  323.2 5.5 collective-permute-start.10
  324.5 5.6 collective-permute-start.11
  328.6 229.0 %all-gather.5.cloned.1.call-start = ((), (), s32[]{:S(2)}) async-start(), calls=%async_computation.7 | async-start | bytes 2162688 | tf_op jit(solution)/shard_map/all_gather | solution.py:119
  426.9 398.5 %reduce-scatter.9.cloned.1.call-start = ((), (), s32[]{:S(2)}) async-start(), calls=%async_computation.8 | async-start | bytes 1179648 | tf_op jit(solution)/shard_map/reduce_scatter | solution.py:124
  427.0 23.5 %collective-permute-start = (f32[32,1,128]{2,1,0:T(1,128)S(1)}, f32[32,1,128]{2,1,0:T(1,128)S(1)}, u32[]{:S(2)}, u32[]{:S(2)}) collective-permute-start(f32[32,1,128]{2,1,0:T(1,128)S(1)} %get-tuple-element.365), channel_id=1, source_target_pairs={{8,0},{16,8},{24,16},{32,24},{40,32},{48,40},{56,48},{64,56},{72,6... | collective-permute-start | bytes 49160 | tf_op jit(solution)/shard_map/ppermute | solution.py:25
  434.7 15.8 %collective-permute-start.1 = (f32[32,1,128]{2,1,0:T(1,128)S(1)}, f32[32,1,128]{2,1,0:T(1,128)S(1)}, u32[]{:S(2)}, u32[]{:S(2)}) collective-permute-start(f32[32,1,128]{2,1,0:T(1,128)S(1)} %get-tuple-element.364), channel_id=1, source_target_pairs={{0,8},{8,16},{16,24},{24,32},{32,40},{40,48},{48,56},{56,64},{64,7... | collective-permute-start | bytes 49160 | tf_op jit(solution)/shard_map/ppermute | solution.py:24
  436.8 4.4 collective-permute-start.5
  439.2 5.0 collective-permute-start.4
  444.2 5.5 collective-permute-start.6
  445.5 4.9 collective-permute-start.7
  450.6 19.1 %copy-start.8 = (f32[32,16,128]{2,1,0:T(8,128)S(1)}, f32[32,16,128]{2,1,0:T(8,128)}, u32[]{:S(2)}) copy-start(f32[32,16,128]{2,1,0:T(8,128)} %param.22) | copy-start | bytes 786436
  450.6 19.1 %copy-start.9 = (f32[32,16,128]{2,1,0:T(8,128)S(1)}, f32[32,16,128]{2,1,0:T(8,128)}, u32[]{:S(2)}) copy-start(f32[32,16,128]{2,1,0:T(8,128)} %param.25) | copy-start | bytes 786436
  450.6 19.1 %copy-start.11 = (f32[16,32,128]{2,0,1:T(8,128)S(1)}, f32[16,32,128]{2,0,1:T(8,128)}, u32[]{:S(2)}) copy-start(f32[16,32,128]{2,0,1:T(8,128)} %get-tuple-element.147) | copy-start | bytes 786436
  450.8 17.1 %collective-permute-start.2 = (f32[32,18,1]{2,1,0:T(8,128)S(1)}, f32[32,18,1]{2,1,0:T(8,128)S(1)}, u32[]{:S(2)}, u32[]{:S(2)}) collective-permute-start(f32[32,18,1]{2,1,0:T(8,128)S(1)} %get-tuple-element.360), channel_id=1, source_target_pairs={{1,0},{2,1},{3,2},{4,3},{5,4},{6,5},{7,6},{9,8},{10,9},{11,10},{12... | collective-permute-start | bytes 6920 | tf_op jit(solution)/shard_map/ppermute | solution.py:25
  452.2 17.2 %collective-permute-start.3 = (f32[32,18,1]{2,1,0:T(8,128)S(1)}, f32[32,18,1]{2,1,0:T(8,128)S(1)}, u32[]{:S(2)}, u32[]{:S(2)}) collective-permute-start(f32[32,18,1]{2,1,0:T(8,128)S(1)} %get-tuple-element.361), channel_id=1, source_target_pairs={{0,1},{1,2},{2,3},{3,4},{4,5},{5,6},{6,7},{8,9},{9,10},{10,11},{11... | collective-permute-start | bytes 6920 | tf_op jit(solution)/shard_map/ppermute | solution.py:24
  456.6 13.5 %copy-start.15 = (f32[32,16,16]{0,2,1:T(8,128)S(1)}, f32[32,16,16]{0,2,1:T(8,128)}, u32[]{:S(2)}) copy-start(f32[32,16,16]{0,2,1:T(8,128)} %param.23) | copy-start | bytes 98308
  456.6 13.5 %copy-start.17 = (f32[32,16,16]{0,2,1:T(8,128)S(1)}, f32[32,16,16]{0,2,1:T(8,128)}, u32[]{:S(2)}) copy-start(f32[32,16,16]{0,2,1:T(8,128)} %param.26) | copy-start | bytes 98308
  562.5 2.9 copy-start
  575.5 2.9 copy-start
  589.1 2.9 copy-start
  602.6 2.9 copy-start
  616.2 2.9 copy-start
  629.8 2.9 copy-start
  643.4 2.9 copy-start
  657.0 2.9 copy-start
  670.6 2.9 copy-start
  684.2 2.9 copy-start
  697.8 2.9 copy-start
  711.4 2.9 copy-start
  725.0 2.9 copy-start
  776.2 157.2 %reduce-scatter.11.cloned.1.call-start = ((), (), s32[]{:S(2)}) async-start(), calls=%async_computation.9 | async-start | bytes 2162688 | tf_op jit(solution)/shard_map/reduce_scatter | solution.py:127
  776.3 5.6 collective-permute-start.12
  778.5 4.2 collective-permute-start.13
  782.8 26.9 %copy-start.6 = (f32[32,4,128]{2,0,1:T(8,128)S(1)}, f32[32,4,128]{2,0,1:T(8,128)}, u32[]{:S(2)}) copy-start(f32[32,4,128]{2,0,1:T(8,128)} %get-tuple-element.350) | copy-start | bytes 196612
  783.0 17.5 %collective-permute-start.14 = (f32[32,18,1]{2,1,0:T(8,128)S(1)}, f32[32,18,1]{2,1,0:T(8,128)S(1)}, u32[]{:S(2)}, u32[]{:S(2)}) collective-permute-start(f32[32,18,1]{2,1,0:T(8,128)S(1)} %get-tuple-element.358), channel_id=1, source_target_pairs={{1,0},{2,1},{3,2},{4,3},{5,4},{6,5},{7,6},{9,8},{10,9},{11,10},{12... | collective-permute-start | bytes 6920 | tf_op jit(solution)/shard_map/ppermute | solution.py:25
  784.3 39.8 %copy-start.10 = (f32[16,32,128]{2,0,1:T(8,128)S(1)}, f32[16,32,128]{2,0,1:T(8,128)}, u32[]{:S(2)}) copy-start(f32[16,32,128]{2,0,1:T(8,128)} %get-tuple-element.150) | copy-start | bytes 786436
  784.3 18.8 %collective-permute-start.15 = (f32[32,18,1]{2,1,0:T(8,128)S(1)}, f32[32,18,1]{2,1,0:T(8,128)S(1)}, u32[]{:S(2)}, u32[]{:S(2)}) collective-permute-start(f32[32,18,1]{2,1,0:T(8,128)S(1)} %get-tuple-element.359), channel_id=1, source_target_pairs={{0,1},{1,2},{2,3},{3,4},{4,5},{5,6},{6,7},{8,9},{9,10},{10,11},{11... | collective-permute-start | bytes 6920 | tf_op jit(solution)/shard_map/ppermute | solution.py:24
  788.6 14.8 %collective-permute-start.16 = (f32[32,1,16]{0,2,1:T(8,128)S(1)}, f32[32,1,16]{0,2,1:T(8,128)S(1)}, u32[]{:S(2)}, u32[]{:S(2)}) collective-permute-start(f32[32,1,16]{0,2,1:T(8,128)S(1)} %get-tuple-element.371), channel_id=1, source_target_pairs={{8,0},{16,8},{24,16},{32,24},{40,32},{48,40},{56,48},{64,56},{72,6... | collective-permute-start | bytes 6152 | tf_op jit(solution)/shard_map/ppermute | solution.py:25
  790.5 12.9 %collective-permute-start.17 = (f32[32,1,16]{0,2,1:T(8,128)S(1)}, f32[32,1,16]{0,2,1:T(8,128)S(1)}, u32[]{:S(2)}, u32[]{:S(2)}) collective-permute-start(f32[32,1,16]{0,2,1:T(8,128)S(1)} %get-tuple-element.370), channel_id=1, source_target_pairs={{0,8},{8,16},{16,24},{24,32},{32,40},{40,48},{48,56},{56,64},{64,7... | collective-permute-start | bytes 6152 | tf_op jit(solution)/shard_map/ppermute | solution.py:24
  803.5 11.8 %collective-permute-start.18 = (f32[32,18,1]{0,2,1:T(1,128)S(1)}, f32[32,18,1]{0,2,1:T(1,128)S(1)}, u32[]{:S(2)}, u32[]{:S(2)}) collective-permute-start(f32[32,18,1]{0,2,1:T(1,128)S(1)} %get-tuple-element.366), channel_id=1, source_target_pairs={{1,0},{2,1},{3,2},{4,3},{5,4},{6,5},{7,6},{9,8},{10,9},{11,10},{12... | collective-permute-start | bytes 6920 | tf_op jit(solution)/shard_map/ppermute | solution.py:25
  804.8 10.6 %collective-permute-start.19 = (f32[32,18,1]{0,2,1:T(1,128)S(1)}, f32[32,18,1]{0,2,1:T(1,128)S(1)}, u32[]{:S(2)}, u32[]{:S(2)}) collective-permute-start(f32[32,18,1]{0,2,1:T(1,128)S(1)} %get-tuple-element.367), channel_id=1, source_target_pairs={{0,1},{1,2},{2,3},{3,4},{4,5},{5,6},{6,7},{8,9},{9,10},{10,11},{11... | collective-permute-start | bytes 6920 | tf_op jit(solution)/shard_map/ppermute | solution.py:24
  809.7 5.7 collective-permute-start.20
  811.9 4.3 collective-permute-start.21
  816.2 9.2 copy-start.16
  816.2 9.2 copy-start.18
  816.2 9.2 copy-start.19
  816.3 6.0 collective-permute-start.22
  817.7 6.3 collective-permute-start.23
  824.2 109.3 %copy-start.22 = (f32[32,4,128]{2,1,0:T(4,128)S(1)}, f32[32,4,128]{2,1,0:T(4,128)}, u32[]{:S(2)}) copy-start(f32[32,4,128]{2,1,0:T(4,128)} %param.27) | copy-start | bytes 196612
  824.2 109.3 %copy-start.23 = (f32[32,4,128]{2,0,1:T(8,128)S(1)}, f32[32,4,128]{2,0,1:T(8,128)}, u32[]{:S(2)}) copy-start(f32[32,4,128]{2,0,1:T(8,128)} %get-tuple-element.351) | copy-start | bytes 196612
  (52 other events, 99.4 us)
Sparse Core Ops, SparseCore 0:
  11.4 84.1 all-gather.2
  314.8 110.3 reduce-scatter.6
  428.0 39.7 reduce-scatter.4
  471.4 86.0 all-gather.4
  776.4 32.5 reduce-scatter.8
  813.5 119.8 reduce-scatter.10
where the time goes:
time: 955 us; the launch traced here: 943 us
  waiting for transfers between devices  346 us (36%)
  matrix products  265 us (28%)
  local copies, waits for them, and re-layouts  129 us (14%)
  starting transfers between devices  69.9 us (7%)
  other arithmetic  58.9 us (6%)
  blocking collectives  58.1 us (6%)
  between operations  14.9 us (2%)
    reduce_scatter x2, waiting for transfers between devices, per_device(): lax.psum_scatter(term_yz, 'gx', scatter_dimension=1, tiled=True)  201 us
    dot_general x32, matrix products, one_row(): jnp.einsum('ch,hzy->czy', w_hidden, back_hidden, preferred_element_type=j...  170 us
    all_gather x2, waiting for transfers between devices, per_device(): whole_yz = lax.all_gather(plane_yz, 'gx', axis=1, tiled=True)  112 us
    dot_general x32, matrix products, one_row(): jnp.einsum('ch,czy->hzy', w_hidden, features, preferred_element_type=jnp....  71 us
    dynamic_update_slice x64, local copies, waits for them, and re-layouts, data_grads(): lax.scan(one_row, start, (target, jnp.moveaxis(plane_xy, 1, 0), jnp.movea...  61.7 us
    all_gather x2, blocking collectives, per_device(): whole_xz = lax.all_gather(plane_xz, 'gy', axis=2, tiled=True)  58.1 us
    sub x32, other arithmetic, one_row(): residual = output - target_row  49.1 us
    ppermute x12, starting transfers between devices, padded_2(): before = lax.ppermute(last, axis, up)  43.9 us
  transfers between devices with their start and end apart: 30, of which 16 were waited for; matrix products, arithmetic and copies ran while one was open for 1% of the time, Pallas kernels for 0%

commit v1 on v0

--- a/solution.py
+++ b/solution.py
@@ -1,6 +1,8 @@
 import jax
 import jax.numpy as jnp
 from jax import lax
+from jax.experimental import pallas as pl
+from jax.experimental.pallas import tpu as pltpu
 from jax.sharding import PartitionSpec as P
 
 STEPS = 2
@@ -12,6 +14,10 @@
 BETA_TWO = 0.99
 LEARN_RATE = 0.01
 EPSILON = 1e-08
+NX = 16
+NB = 16
+F32 = jnp.float32
+BF = jnp.bfloat16
 
 
 def padded_2(x, sides, width):
@@ -52,41 +58,89 @@
     )
 
 
-def data_grads(target, plane_xy, whole_xz, whole_yz, w_hidden, b_hidden, w_output, b_output):
-    weights_out = w_output.astype(jnp.float32)
-
-    def one_row(running, inputs):
-        target_row, row_xy, row_xz = inputs
-        cross = row_xz[:, :, None] * whole_yz
-        features = (row_xy[:, None, :] * cross).astype(jnp.bfloat16)
-        preact = (
-            jnp.einsum("ch,czy->hzy", w_hidden, features, preferred_element_type=jnp.float32)
-            + b_hidden[:, None, None]
-        )
-        sigma = jax.nn.sigmoid(preact)
-        hidden = (preact * sigma).astype(jnp.bfloat16)
-        output = (
-            jnp.einsum("h,hzy->zy", w_output, hidden, preferred_element_type=jnp.float32)
-            + b_output[0]
-        )
-        residual = output - target_row
-        back_hidden = (
-            weights_out[:, None, None] * residual[None] * (sigma * (1.0 + preact * (1.0 - sigma)))
-        ).astype(jnp.bfloat16)
-        back_feature = jnp.einsum(
-            "ch,hzy->czy", w_hidden, back_hidden, preferred_element_type=jnp.float32
-        )
-        grad_row_xy = jnp.sum(back_feature * cross, axis=1)
-        with_xy = back_feature * row_xy[:, None, :]
-        grad_row_xz = jnp.sum(with_xy * whole_yz, axis=2)
-        running = running + with_xy * row_xz[:, :, None]
-        return (running, (grad_row_xy, grad_row_xz))
-
-    start = jnp.zeros(whole_yz.shape, jnp.float32)
-    grad_yz, (rows_xy, rows_xz) = lax.scan(
-        one_row, start, (target, jnp.moveaxis(plane_xy, 1, 0), jnp.moveaxis(whole_xz, 1, 0))
-    )
-    return (jnp.moveaxis(rows_xy, 0, 1), jnp.moveaxis(rows_xz, 0, 1), grad_yz)
+def grad_block(zb, tgt, xy, xz, yz, w1, w2, wo, bh, wv, b0, accxy, gxz, gyz, fbuf, dbuf, rbuf):
+    wide = NX * 128
+    xt = jnp.transpose(xz[zb])
+    h1 = xt.astype(BF)
+    r1 = xt - h1.astype(F32)
+    h2 = r1.astype(BF)
+    h3 = (r1 - h2.astype(F32)).astype(BF)
+    parts = jnp.concatenate([h1, h2, h3], axis=1)
+    place = lax.broadcasted_iota(jnp.int32, (3 * NX, 128), 0) % NX
+    yzt = yz[pl.ds(zb * 8, 8)].reshape(256, 128)
+    for x in range(NX):
+        col = jnp.dot(parts, (place == x).astype(BF), preferred_element_type=F32)
+        f = ((col * yzt).reshape(8, 32, 128) * xy[x][None]).reshape(256, 128)
+        fbuf[:, x * 128 : (x + 1) * 128] = f
+    pre = jnp.dot(w1[...], fbuf[...].astype(BF), preferred_element_type=F32)
+    q = pre.reshape(8, 32, wide) + jnp.concatenate([bh[...]] * NX, axis=-1)[None]
+    u = 1.0 + jnp.tanh(q)
+    h = q * u
+    dbuf[...] = (u + h * (2.0 - u)) * jnp.concatenate([wv[...]] * NX, axis=-1)[None]
+    out = jnp.dot(wo[...], h.reshape(256, wide).astype(BF), preferred_element_type=F32)[:8]
+    for x in range(NX):
+        rbuf[:, x * 128 : (x + 1) * 128] = (
+            out[:, x * 128 : (x + 1) * 128] + b0 - tgt[x, pl.ds(zb * 8, 8), :]
+        )
+    d = (dbuf[...] * rbuf[...][:, None, :]).reshape(256, wide)
+    s = jnp.dot(w2[...], d.astype(BF), preferred_element_type=F32) * fbuf[...]
+    acc = None
+    for x in range(NX):
+        sx = s[:, x * 128 : (x + 1) * 128]
+        acc = sx if acc is None else acc + sx
+        accxy[x] += jnp.sum(sx.reshape(8, 32, 128), axis=0)
+        gxz[zb, x : x + 1, :] = jnp.sum(sx, axis=-1).reshape(1, 256)
+    gyz[pl.ds(zb * 8, 8)] = acc.reshape(8, 32, 128)
+
+
+def grad_kernel(tgt, xy, xz, yz, w1, w2, wo, bh, wv, bo, gxy, gxz, gyz, fbuf, dbuf, rbuf):
+    gxy[...] = jnp.zeros_like(gxy)
+    b0 = bo[0]
+
+    def step(zb, carry):
+        grad_block(zb, tgt, xy, xz, yz, w1, w2, wo, bh, wv, b0, gxy, gxz, gyz, fbuf, dbuf, rbuf)
+        return carry
+
+    lax.fori_loop(0, NB, step, 0)
+
+
+def weights(w_hidden, b_hidden, w_output):
+    eye = jnp.eye(8, dtype=F32)
+    wf = w_hidden.astype(F32)
+    w1 = jnp.kron(eye, 0.5 * wf.T).astype(BF)
+    w2 = jnp.kron(eye, wf).astype(BF)
+    wof = w_output.astype(F32)
+    wo = jnp.pad(jnp.kron(eye, wof[None, :]), ((0, 8), (0, 0))).astype(BF)
+    bh = jnp.broadcast_to((0.5 * b_hidden)[:, None], (32, 128))
+    wv = jnp.broadcast_to((0.5 * wof)[:, None], (32, 128))
+    return w1, w2, wo, bh, wv
+
+
+def data_grads(target, plane_xy, whole_xz, whole_yz, ws, b_output):
+    xy = jnp.transpose(plane_xy, (1, 0, 2))
+    xz = jnp.transpose(whole_xz.reshape(32, NX, NB, 8), (2, 1, 3, 0)).reshape(NB, NX, 256)
+    yz = jnp.transpose(whole_yz, (1, 0, 2))
+    vm = pl.BlockSpec(memory_space=pltpu.VMEM)
+    gxy, gxz, gyz = pl.pallas_call(
+        grad_kernel,
+        out_shape=[
+            jax.ShapeDtypeStruct((NX, 32, 128), F32),
+            jax.ShapeDtypeStruct((NB, NX, 256), F32),
+            jax.ShapeDtypeStruct((NB * 8, 32, 128), F32),
+        ],
+        in_specs=[vm] * 9 + [pl.BlockSpec(memory_space=pltpu.SMEM)],
+        out_specs=[vm] * 3,
+        scratch_shapes=[
+            pltpu.VMEM((256, NX * 128), F32),
+            pltpu.VMEM((8, 32, NX * 128), F32),
+            pltpu.VMEM((8, NX * 128), F32),
+        ],
+        compiler_params=pltpu.CompilerParams(vmem_limit_bytes=48 * 2**20),
+    )(target, xy, xz, yz, *ws, b_output)
+    gxy = jnp.transpose(gxy, (1, 0, 2)) / plane_xy
+    gxz = jnp.transpose((gxz / xz).reshape(NB, NX, 8, 32), (3, 1, 0, 2)).reshape(32, NX, NB * 8)
+    gyz = jnp.transpose(gyz / yz, (1, 0, 2))
+    return gxy, gxz, gyz
 
 
 def adam(plane, first, second, grads, count):
@@ -114,11 +168,12 @@
     w_output,
     b_output,
 ):
+    ws = weights(w_hidden, b_hidden, w_output)
     for iteration in range(STEPS):
         whole_xz = lax.all_gather(plane_xz, "gy", axis=2, tiled=True)
         whole_yz = lax.all_gather(plane_yz, "gx", axis=1, tiled=True)
         grad_xy, term_xz, term_yz = data_grads(
-            target, plane_xy, whole_xz, whole_yz, w_hidden, b_hidden, w_output, b_output
+            target, plane_xy, whole_xz, whole_yz, ws, b_output
         )
         grad_xy = grad_xy + smooth(plane_xy)
         grad_xz = lax.psum_scatter(term_xz, "gy", scatter_dimension=2, tiled=True) + smooth(

time: 955 us -> 589 us (0.62)
  matrix products: 265 us -> 0 us
  local copies, waits for them, and re-layouts: 129 us -> 26.2 us
  Pallas kernels: 0 us -> 71.2 us
  other arithmetic: 58.9 us -> 17.9 us
  waiting for transfers between devices: 346 us -> 325 us
    dot_general x96 -> x0, matrix products: 265 us -> none  [the longest x32 170 us: one_row(): jnp.einsum('ch,hzy->czy', w_hidden, back_hidden, preferred_element_type=j...]
    pallas_call x0 -> x2, Pallas kernels: none -> 71.2 us  [data_grads(): pl.pallas_call(grad_kernel, out_shape=[jax.ShapeDtypeStruct((NX, 32, 128)...]
    dynamic_update_slice x64 -> x0, local copies, waits for them, and re-layouts: 61.7 us -> none  [data_grads(): lax.scan(one_row, start, (target, jnp.moveaxis(plane_xy, 1, 0), jnp.movea...]
    sub x32 -> x0, other arithmetic: 49.1 us -> none  [one_row(): residual = output - target_row]
    mul x48 -> x5, local copies, waits for them, and re-layouts: 38.5 us -> 0.97 us  [the longest x4 0.9 us: weights(): wo = jnp.pad(jnp.kron(eye, wof[None, :]), ((0, 8), (0, 0))).astype(BF)]
    while x128 -> x0, local copies, waits for them, and re-layouts: 19.4 us -> none
  transfers between devices with their start and end apart: 30 -> 30, of which waited for: 16 -> 15; matrix products, arithmetic and copies ran while one was open for 1% -> 5% of each run, Pallas kernels for 0% -> 0%
where the time goes in v1:
time: 589 us; the launch traced here: 583 us
  waiting for transfers between devices  325 us (55%)
  starting transfers between devices  72.9 us (12%)
  Pallas kernels  71.2 us (12%)
  blocking collectives  54.3 us (9%)
  local copies, waits for them, and re-layouts  26.2 us (4%)
  other arithmetic  17.9 us (3%)
  between operations  15.7 us (3%)
    reduce_scatter x2, waiting for transfers between devices, per_device(): lax.psum_scatter(term_yz, 'gx', scatter_dimension=1, tiled=True)  197 us
    all_gather x2, waiting for transfers between devices, per_device(): whole_yz = lax.all_gather(plane_yz, 'gx', axis=1, tiled=True)  103 us
    pallas_call x2, Pallas kernels, data_grads(): pl.pallas_call(grad_kernel, out_shape=[jax.ShapeDtypeStruct((NX, 32, 128)...  71.2 us
    all_gather x2, blocking collectives, per_device(): whole_xz = lax.all_gather(plane_xz, 'gy', axis=2, tiled=True)  54.3 us
    ppermute x12, starting transfers between devices, padded_2(): before = lax.ppermute(last, axis, up)  46.5 us
    ppermute x12, starting transfers between devices, padded_2(): after = lax.ppermute(first, axis, down)  26.1 us
    ppermute x12, waiting for transfers between devices, padded_2(): after = lax.ppermute(first, axis, down)  17.6 us
  transfers between devices with their start and end apart: 30, of which 15 were waited for; matrix products, arithmetic and copies ran while one was open for 5% of the time, Pallas kernels for 0%

profile of v1, /device:TPU:1, one launch (start us, length us, event | category | flops | bytes accessed | tf_op | source)
XLA Modules:
  0.0 583.3 jit_solution(6633348932671816285)
XLA Ops:
  7.2 1.5 copy.56
  8.8 1.0 copy.65
  10.4 4.9 collective-permute-start.1
  17.7 26.5 %all_gather.12 = f32[32,16,128]{0,2,1:T(8,128)S(1)} all-gather(f32[32,16,16]{0,2,1:T(8,128)} %param.16), channel_id=1, replica_groups=mesh['gx'=32,'gy'=8] {'gy'}, dimensions={2}, use_global_device_ids=true | all-gather | bytes 294912 | tf_op jit(solution)/shard_map/all_gather | solution.py:173
  44.3 1.3 multiply_convert_fusion
  45.7 1.5 convert_element_type.31.w1
  47.2 1.4 convert_element_type.33.w2
  50.4 45.2 %all-gather.3.cloned.1.call-done = f32[32,128,128]{2,0,1:T(8,128)} async-done(((f32[32,4,128]{2,0,1:T(8,128)}), f32[32,128,128]{2,0,1:T(8,128)}) %all-gather.3.cloned.1.call-update) | async-done | bytes 2097168 | tf_op jit(solution)/shard_map/all_gather | solution.py:174
  95.7 35.6 %shard_map.205 = (f32[16,32,128]{2,1,0:T(8,128)S(1)}, f32[16,16,256]{2,1,0:T(8,128)S(1)}, f32[128,32,128]{2,1,0:T(8,128)S(1)}) custom-call(f32[16,128,128]{2,1,0:T(8,128)S(1)} %copy-done, f32[16,32,128]{2,1,0:T(8,128)S(1)} %get-tuple-element.60.xy, f32[16,16,256]{2,1,0:T(8,128)S(1)} %reshape.110.xz, f32[128,32,128]{2,1,0:T(8,128)} %bitcast.52, ...), custom_call_target="tpu_custom_call" | custom-call | tf_op jit(solution)/shard_map/pallas_call | solution.py:124
  131.4 1.8 divide_bitcast_fusion.1
  133.3 0.8 copy-done.13
  134.0 2.5 collective-permute-start.9
  136.6 1.9 collective-permute-start.8
  138.6 3.0 collective-permute-done.8
  142.4 1.3 collective-permute-start.10
  143.6 4.7 collective-permute-start.11
  148.4 1.3 reshape.111
  149.7 2.4 copy_bitcast_fusion.2
  152.2 1.0 fusion.23
  153.2 90.4 %reduce-scatter.7.cloned.1.call-done = f32[32,4,128]{2,0,1:T(8,128)} async-done(((f32[32,128,128]{2,0,1:T(8,128)}), f32[32,4,128]{2,0,1:T(8,128)}) %reduce-scatter.7.cloned.1.call-update) | async-done | bytes 65552 | tf_op jit(solution)/shard_map/reduce_scatter | solution.py:182
  243.7 1.6 divide_subtract_fusion.5
  245.3 7.8 %collective-permute-start = (f32[32,1,128]{2,0,1:T(8,128)S(1)}, f32[32,1,128]{2,0,1:T(8,128)S(1)}, u32[]{:S(2)}, u32[]{:S(2)}) collective-permute-start(f32[32,1,128]{2,0,1:T(8,128)S(1)} %copy-done.27), channel_id=1, source_target_pairs={{8,0},{16,8},{24,16},{32,24},{40,32},{48,40},{56,48},{64,56},{72,6... | collective-permute-start | bytes 49160 | tf_op jit(solution)/shard_map/ppermute | solution.py:31
  253.2 2.1 collective-permute-start.5
  255.3 2.3 collective-permute-start.4
  257.7 2.7 collective-permute-done.4
  260.4 1.3 collective-permute-start.6
  261.7 4.0 collective-permute-start.7
  267.4 1.3 collective-permute-start.2
  268.7 4.7 collective-permute-start.3
  273.5 8.4 %collective-permute-done.2 = f32[32,18,1]{2,0,1:T(8,128)S(1)} collective-permute-done((f32[32,18,1]{2,0,1:T(8,128)S(1)}, f32[32,18,1]{2,0,1:T(8,128)S(1)}, u32[]{:S(2)}, u32[]{:S(2)}) %collective-permute-start.2) | collective-permute-done | bytes 2336 | tf_op jit(solution)/shard_map/ppermute | solution.py:31
  281.9 2.1 collective-permute-done.3
  284.2 1.1 divide_subtract_fusion.1
  285.3 1.0 reduce-scatter.5.cloned.1.call-done
  286.2 1.1 divide_subtract_fusion.3
  287.4 27.8 %all_gather.14 = f32[32,16,128]{0,2,1:T(8,128)S(1)} all-gather(f32[32,16,16]{0,2,1:T(8,128)S(1)} %get-tuple-element.50), channel_id=1, replica_groups=mesh['gx'=32,'gy'=8] {'gy'}, dimensions={2}, use_global_device_ids=true | all-gather | bytes 294912 | tf_op jit(solution)/shard_map/all_gather | solution.py:173
  315.1 1.1 copy_bitcast_fusion.1
  316.2 1.5 reshape.114.xz
  317.8 58.2 %all-gather.5.cloned.1.call-done = f32[32,128,128]{2,0,1:T(8,128)} async-done(((f32[32,4,128]{2,0,1:T(8,128)}), f32[32,128,128]{2,0,1:T(8,128)}) %all-gather.5.cloned.1.call-update) | async-done | bytes 2097168 | tf_op jit(solution)/shard_map/all_gather | solution.py:174
  376.0 35.5 %shard_map.206 = (f32[16,32,128]{2,1,0:T(8,128)S(1)}, f32[16,16,256]{2,1,0:T(8,128)S(1)}, f32[128,32,128]{2,1,0:T(8,128)S(1)}) custom-call(f32[16,128,128]{2,1,0:T(8,128)S(1)} %copy-done, f32[16,32,128]{2,1,0:T(8,128)S(1)} %bitcast.50, f32[16,16,256]{2,1,0:T(8,128)S(1)} %reshape.114.xz, f32[128,32,128]{2,1,0:T(8,128)} %bitcast.51, ...), custom_call_target="tpu_custom_call" | custom-call | tf_op jit(solution)/shard_map/pallas_call | solution.py:124
  411.5 1.3 copy-done.1
  412.9 1.2 reshape.115
  414.2 2.3 copy_bitcast_fusion
  416.6 2.2 collective-permute-start.12
  418.8 3.4 collective-permute-start.13
  422.2 3.4 divide_bitcast_fusion
  425.9 1.4 collective-permute-start.14
  427.4 4.2 collective-permute-start.15
  431.7 1.9 collective-permute-start.16
  433.6 3.6 collective-permute-start.17
  437.2 3.2 collective-permute-done.14
  440.4 0.9 collective-permute-done.15
  441.6 1.3 collective-permute-start.18
  442.9 4.9 collective-permute-start.19
  447.9 2.1 collective-permute-start.20
  450.1 3.4 collective-permute-start.21
  454.5 1.3 collective-permute-start.22
  455.8 4.1 collective-permute-start.23
  460.3 1.8 collective-permute-done.23
  462.7 0.9 copy.77
  463.5 0.9 copy.79
  464.4 0.9 copy.81
  465.2 1.8 divide_subtract_fusion.2
  467.0 106.4 %reduce-scatter.11.cloned.1.call-done = f32[32,4,128]{2,0,1:T(8,128)} async-done(((f32[32,128,128]{2,0,1:T(8,128)}), f32[32,4,128]{2,0,1:T(8,128)}) %reduce-scatter.11.cloned.1.call-update) | async-done | bytes 65552 | tf_op jit(solution)/shard_map/reduce_scatter | solution.py:182
  573.4 1.0 divide_subtract_fusion.4
  (156 shorter events, 12.2 us)
Async XLA Ops:
  7.2 37.1 %copy-start.32 = (bf16[32]{0:T(256)(128)(2,1)S(1)}, bf16[32]{0:T(256)(128)(2,1)}, u32[]{:S(2)}) copy-start(bf16[32]{0:T(256)(128)(2,1)} %param.26) | copy-start | bytes 196
  7.2 88.4 %all-gather.3.cloned.1.call-start = ((), (), s32[]{:S(2)}) async-start(), calls=%async_computation.4 | async-start | bytes 2162688 | tf_op jit(solution)/shard_map/all_gather | solution.py:174
  8.7 234.9 %reduce-scatter.7.cloned.1.call-start = ((), (), s32[]{:S(2)}) async-start(), calls=%async_computation.6 | async-start | bytes 2162688 | tf_op jit(solution)/shard_map/reduce_scatter | solution.py:182
  10.4 39.2 %collective-permute-start.1 = (f32[32,1,128]{2,0,1:T(8,128)S(1)}, f32[32,1,128]{2,0,1:T(8,128)S(1)}, u32[]{:S(2)}, u32[]{:S(2)}) collective-permute-start(f32[32,1,128]{2,0,1:T(8,128)S(1)} %get-tuple-element.63), channel_id=1, source_target_pairs={{0,8},{8,16},{16,24},{24,32},{32,40},{40,48},{48,56},{56,64},{64,7... | collective-permute-start | bytes 49160 | tf_op jit(solution)/shard_map/ppermute | solution.py:30
  17.7 27.9 %copy-start.33 = (f32[32]{0:T(128)S(1)}, f32[32]{0:T(128)}, u32[]{:S(2)}) copy-start(f32[32]{0:T(128)} %param.25) | copy-start | bytes 388
  45.6 4.7 copy-start.5
  45.7 50.0 %copy-start = (f32[16,128,128]{2,1,0:T(8,128)S(1)}, f32[16,128,128]{2,1,0:T(8,128)}, u32[]{:S(2)}) copy-start(f32[16,128,128]{2,1,0:T(8,128)} %tgt.3) | copy-start | bytes 3145732
  49.7 0.6 copy-start.25
  95.6 35.8 %copy-start.3 = (f32[32,128,128]{2,0,1:T(8,128)S(1)}, f32[32,128,128]{2,0,1:T(8,128)}, u32[]{:S(2)}) copy-start(f32[32,128,128]{2,0,1:T(8,128)} %all-gather.3.cloned.1.call-done) | copy-start | bytes 6291460
  133.2 0.8 copy-start.13
  133.2 5.4 copy-start.14
  133.2 153.0 %reduce-scatter.5.cloned.1.call-start = ((), (), s32[]{:S(2)}) async-start(), calls=%async_computation.5 | async-start | bytes 1179648 | tf_op jit(solution)/shard_map/reduce_scatter | solution.py:179
  134.0 4.5 collective-permute-start.9
  136.6 5.1 collective-permute-start.8
  138.5 13.6 %copy-start.28 = (f32[5]{0:T(128)}, f32[5]{0:T(128)S(1)}, u32[]{:S(2)}) copy-start(f32[5]{0:T(128)S(1)} %or_select_fusion) | copy-start | bytes 64
  141.6 6.7 %copy-start.23 = (f32[32,1,128]{2,0,1:T(8,128)}, f32[32,1,128]{2,0,1:T(8,128)S(1)}, u32[]{:S(2)}) copy-start(f32[32,1,128]{2,0,1:T(8,128)S(1)} %collective-permute-done.8) | copy-start | bytes 49156
  142.4 9.9 %collective-permute-start.10 = (f32[32,6,1]{2,0,1:T(8,128)}, f32[32,6,1]{2,0,1:T(8,128)}, u32[]{:S(2)}, u32[]{:S(2)}) collective-permute-start(f32[32,6,1]{2,0,1:T(8,128)} %get-tuple-element.74), channel_id=1, source_target_pairs={{1,0},{2,1},{3,2},{4,3},{5,4},{6,5},{7,6},{9,8},{10,9},{11,10},{12... | collective-permute-start | bytes 2312 | tf_op jit(solution)/shard_map/ppermute | solution.py:31
  143.6 8.6 %collective-permute-start.11 = (f32[32,6,1]{2,0,1:T(8,128)}, f32[32,6,1]{2,0,1:T(8,128)}, u32[]{:S(2)}, u32[]{:S(2)}) collective-permute-start(f32[32,6,1]{2,0,1:T(8,128)} %get-tuple-element.75), channel_id=1, source_target_pairs={{0,1},{1,2},{2,3},{3,4},{4,5},{5,6},{6,7},{8,9},{9,10},{10,11},{11... | collective-permute-start | bytes 2312 | tf_op jit(solution)/shard_map/ppermute | solution.py:30
  149.6 2.5 copy-start.24
  149.6 94.0 %copy-start.15 = (f32[32,4,128]{2,1,0:T(4,128)S(1)}, f32[32,4,128]{2,1,0:T(4,128)}, u32[]{:S(2)}) copy-start(f32[32,4,128]{2,1,0:T(4,128)} %param.17) | copy-start | bytes 196612
  149.6 94.0 %copy-start.18 = (f32[32,4,128]{2,1,0:T(4,128)S(1)}, f32[32,4,128]{2,1,0:T(4,128)}, u32[]{:S(2)}) copy-start(f32[32,4,128]{2,1,0:T(4,128)} %param.20) | copy-start | bytes 196612
  149.6 94.0 %copy-start.20 = (f32[32,4,128]{2,1,0:T(4,128)S(1)}, f32[32,4,128]{2,1,0:T(4,128)}, u32[]{:S(2)}) copy-start(f32[32,4,128]{2,1,0:T(4,128)} %param.23) | copy-start | bytes 196612
  149.6 95.7 %copy-start.27 = (f32[32,1,128]{2,0,1:T(8,128)S(1)}, f32[32,1,128]{2,0,1:T(8,128)}, u32[]{:S(2)}) copy-start(f32[32,1,128]{2,0,1:T(8,128)} %get-tuple-element.62) | copy-start | bytes 49156
  149.6 103.5 %copy-start.6 = (f32[32,16,16]{0,2,1:T(8,128)S(1)}, f32[32,16,16]{0,2,1:T(8,128)}, u32[]{:S(2)}) copy-start(f32[32,16,16]{0,2,1:T(8,128)} %param.16) | copy-start | bytes 98308
  152.0 121.3 %copy-start.26 = (f32[32,1,128]{2,0,1:T(8,128)S(1)}, f32[32,1,128]{2,0,1:T(8,128)}, u32[]{:S(2)}) copy-start(f32[32,1,128]{2,0,1:T(8,128)} %copy-done.25) | copy-start | bytes 49156
  152.1 223.9 %all-gather.5.cloned.1.call-start = ((), (), s32[]{:S(2)}) async-start(), calls=%async_computation.7 | async-start | bytes 2162688 | tf_op jit(solution)/shard_map/all_gather | solution.py:174
  245.3 220.0 %reduce-scatter.9.cloned.1.call-start = ((), (), s32[]{:S(2)}) async-start(), calls=%async_computation.8 | async-start | bytes 1179648 | tf_op jit(solution)/shard_map/reduce_scatter | solution.py:179
  245.3 21.9 %collective-permute-start = (f32[32,1,128]{2,0,1:T(8,128)S(1)}, f32[32,1,128]{2,0,1:T(8,128)S(1)}, u32[]{:S(2)}, u32[]{:S(2)}) collective-permute-start(f32[32,1,128]{2,0,1:T(8,128)S(1)} %copy-done.27), channel_id=1, source_target_pairs={{8,0},{16,8},{24,16},{32,24},{40,32},{48,40},{56,48},{64,56},{72,6... | collective-permute-start | bytes 49160 | tf_op jit(solution)/shard_map/ppermute | solution.py:31
  253.2 4.5 collective-permute-start.5
  255.3 28.9 %copy-start.8 = (f32[32,16,128]{2,1,0:T(8,128)S(1)}, f32[32,16,128]{2,1,0:T(8,128)}, u32[]{:S(2)}) copy-start(f32[32,16,128]{2,1,0:T(8,128)} %param.18) | copy-start | bytes 786436
  255.3 28.9 %copy-start.10 = (f32[32,16,128]{2,1,0:T(8,128)S(1)}, f32[32,16,128]{2,1,0:T(8,128)}, u32[]{:S(2)}) copy-start(f32[32,16,128]{2,1,0:T(8,128)} %param.21) | copy-start | bytes 786436
  255.3 5.1 collective-permute-start.4
  257.7 27.6 %copy-start.30 = (f32[17]{0:T(128)}, f32[17]{0:T(128)S(1)}, u32[]{:S(2)}) copy-start(f32[17]{0:T(128)S(1)} %or_select_fusion.1) | copy-start | bytes 208
  260.4 5.4 collective-permute-start.6
  261.7 4.8 collective-permute-start.7
  267.4 14.5 %collective-permute-start.2 = (f32[32,18,1]{2,0,1:T(8,128)S(1)}, f32[32,18,1]{2,0,1:T(8,128)S(1)}, u32[]{:S(2)}, u32[]{:S(2)}) collective-permute-start(f32[32,18,1]{2,0,1:T(8,128)S(1)} %get-tuple-element.56), channel_id=1, source_target_pairs={{1,0},{2,1},{3,2},{4,3},{5,4},{6,5},{7,6},{9,8},{10,9},{11,10},{12... | collective-permute-start | bytes 6920 | tf_op jit(solution)/shard_map/ppermute | solution.py:31
  268.7 15.2 %collective-permute-start.3 = (f32[32,18,1]{2,0,1:T(8,128)S(1)}, f32[32,18,1]{2,0,1:T(8,128)S(1)}, u32[]{:S(2)}, u32[]{:S(2)}) collective-permute-start(f32[32,18,1]{2,0,1:T(8,128)S(1)} %get-tuple-element.57), channel_id=1, source_target_pairs={{0,1},{1,2},{2,3},{3,4},{4,5},{5,6},{6,7},{8,9},{9,10},{10,11},{11... | collective-permute-start | bytes 6920 | tf_op jit(solution)/shard_map/ppermute | solution.py:30
  273.5 12.8 %copy-start.7 = (f32[32,16,17]{0,2,1:T(8,128)S(1)}, f32[32,16,17]{0,2,1:T(8,128)}, u32[]{:S(2)}) copy-start(f32[32,16,17]{0,2,1:T(8,128)} %fusion.14) | copy-start | bytes 104452
  273.5 12.7 %copy-start.16 = (f32[32,16,16]{0,2,1:T(8,128)S(1)}, f32[32,16,16]{0,2,1:T(8,128)}, u32[]{:S(2)}) copy-start(f32[32,16,16]{0,2,1:T(8,128)} %param.19) | copy-start | bytes 98308
  411.5 1.4 copy-start.1
  412.9 9.2 %copy-start.2 = (f32[128,32,128]{2,1,0:T(8,128)S(1)}, f32[128,32,128]{2,1,0:T(8,128)}, u32[]{:S(2)}) copy-start(f32[128,32,128]{2,1,0:T(8,128)} %copy-done.1) | copy-start | bytes 6291460
  416.5 156.9 %reduce-scatter.11.cloned.1.call-start = ((), (), s32[]{:S(2)}) async-start(), calls=%async_computation.9 | async-start | bytes 2162688 | tf_op jit(solution)/shard_map/reduce_scatter | solution.py:182
  416.6 9.1 %collective-permute-start.12 = (f32[32,1,128]{2,0,1:T(8,128)S(1)}, f32[32,1,128]{2,0,1:T(8,128)S(1)}, u32[]{:S(2)}, u32[]{:S(2)}) collective-permute-start(f32[32,1,128]{2,0,1:T(8,128)S(1)} %get-tuple-element.59), channel_id=1, source_target_pairs={{8,0},{16,8},{24,16},{32,24},{40,32},{48,40},{56,48},{64,56},{72,6... | collective-permute-start | bytes 49160 | tf_op jit(solution)/shard_map/ppermute | solution.py:31
  418.8 6.9 %collective-permute-start.13 = (f32[32,1,128]{2,0,1:T(8,128)S(1)}, f32[32,1,128]{2,0,1:T(8,128)S(1)}, u32[]{:S(2)}, u32[]{:S(2)}) collective-permute-start(f32[32,1,128]{2,0,1:T(8,128)S(1)} %get-tuple-element.58), channel_id=1, source_target_pairs={{0,8},{8,16},{16,24},{24,32},{32,40},{40,48},{48,56},{56,64},{64,7... | collective-permute-start | bytes 49160 | tf_op jit(solution)/shard_map/ppermute | solution.py:30
  425.7 22.3 %copy-start.4 = (f32[32,4,128]{2,0,1:T(8,128)S(1)}, f32[32,4,128]{2,0,1:T(8,128)}, u32[]{:S(2)}) copy-start(f32[32,4,128]{2,0,1:T(8,128)} %get-tuple-element.48) | copy-start | bytes 196612
  425.7 27.9 %copy-start.31 = (f32[17]{0:T(128)S(1)}, f32[17]{0:T(128)}, u32[]{:S(2)}) copy-start(f32[17]{0:T(128)} %copy-done.30) | copy-start | bytes 208
  425.7 34.1 %copy-start.29 = (f32[5]{0:T(128)S(1)}, f32[5]{0:T(128)}, u32[]{:S(2)}) copy-start(f32[5]{0:T(128)} %copy-done.28) | copy-start | bytes 64
  425.9 36.3 %copy-start.9 = (f32[32,16,128]{2,1,0:T(8,128)S(1)}, f32[32,16,128]{2,1,0:T(8,128)}, u32[]{:S(2)}) copy-start(f32[32,16,128]{2,1,0:T(8,128)} %param.18) | copy-start | bytes 786436
  425.9 36.3 %copy-start.11 = (f32[32,16,128]{2,1,0:T(8,128)S(1)}, f32[32,16,128]{2,1,0:T(8,128)}, u32[]{:S(2)}) copy-start(f32[32,16,128]{2,1,0:T(8,128)} %param.21) | copy-start | bytes 786436
  425.9 36.3 %copy-start.12 = (f32[32,16,128]{2,0,1:T(8,128)S(1)}, f32[32,16,128]{2,0,1:T(8,128)}, u32[]{:S(2)}) copy-start(f32[32,16,128]{2,0,1:T(8,128)} %get-tuple-element.53) | copy-start | bytes 786436
  425.9 14.5 %collective-permute-start.14 = (f32[32,18,1]{2,0,1:T(8,128)S(1)}, f32[32,18,1]{2,0,1:T(8,128)S(1)}, u32[]{:S(2)}, u32[]{:S(2)}) collective-permute-start(f32[32,18,1]{2,0,1:T(8,128)S(1)} %get-tuple-element.54), channel_id=1, source_target_pairs={{1,0},{2,1},{3,2},{4,3},{5,4},{6,5},{7,6},{9,8},{10,9},{11,10},{12... | collective-permute-start | bytes 6920 | tf_op jit(solution)/shard_map/ppermute | solution.py:31
  427.4 14.0 %collective-permute-start.15 = (f32[32,18,1]{2,0,1:T(8,128)S(1)}, f32[32,18,1]{2,0,1:T(8,128)S(1)}, u32[]{:S(2)}, u32[]{:S(2)}) collective-permute-start(f32[32,18,1]{2,0,1:T(8,128)S(1)} %get-tuple-element.55), channel_id=1, source_target_pairs={{0,1},{1,2},{2,3},{3,4},{4,5},{5,6},{6,7},{8,9},{9,10},{10,11},{11... | collective-permute-start | bytes 6920 | tf_op jit(solution)/shard_map/ppermute | solution.py:30
  431.7 9.9 %collective-permute-start.16 = (f32[32,1,16]{0,2,1:T(8,128)S(1)}, f32[32,1,16]{0,2,1:T(8,128)S(1)}, u32[]{:S(2)}, u32[]{:S(2)}) collective-permute-start(f32[32,1,16]{0,2,1:T(8,128)S(1)} %get-tuple-element.69), channel_id=1, source_target_pairs={{8,0},{16,8},{24,16},{32,24},{40,32},{48,40},{56,48},{64,56},{72,6... | collective-permute-start | bytes 6152 | tf_op jit(solution)/shard_map/ppermute | solution.py:31
  433.6 8.0 %collective-permute-start.17 = (f32[32,1,16]{0,2,1:T(8,128)S(1)}, f32[32,1,16]{0,2,1:T(8,128)S(1)}, u32[]{:S(2)}, u32[]{:S(2)}) collective-permute-start(f32[32,1,16]{0,2,1:T(8,128)S(1)} %get-tuple-element.68), channel_id=1, source_target_pairs={{0,8},{8,16},{16,24},{24,32},{32,40},{40,48},{48,56},{56,64},{64,7... | collective-permute-start | bytes 6152 | tf_op jit(solution)/shard_map/ppermute | solution.py:30
  441.6 11.9 %collective-permute-start.18 = (f32[32,18,1]{0,2,1:T(1,128)S(1)}, f32[32,18,1]{0,2,1:T(1,128)S(1)}, u32[]{:S(2)}, u32[]{:S(2)}) collective-permute-start(f32[32,18,1]{0,2,1:T(1,128)S(1)} %get-tuple-element.64), channel_id=1, source_target_pairs={{1,0},{2,1},{3,2},{4,3},{5,4},{6,5},{7,6},{9,8},{10,9},{11,10},{12... | collective-permute-start | bytes 6920 | tf_op jit(solution)/shard_map/ppermute | solution.py:31
  442.9 10.6 %collective-permute-start.19 = (f32[32,18,1]{0,2,1:T(1,128)S(1)}, f32[32,18,1]{0,2,1:T(1,128)S(1)}, u32[]{:S(2)}, u32[]{:S(2)}) collective-permute-start(f32[32,18,1]{0,2,1:T(1,128)S(1)} %get-tuple-element.65), channel_id=1, source_target_pairs={{0,1},{1,2},{2,3},{3,4},{4,5},{5,6},{6,7},{8,9},{9,10},{10,11},{11... | collective-permute-start | bytes 6920 | tf_op jit(solution)/shard_map/ppermute | solution.py:30
  447.9 5.7 collective-permute-start.20
  450.1 4.3 collective-permute-start.21
  454.5 5.8 %collective-permute-start.22 = (f32[32,6,1]{2,0,1:T(8,128)S(1)}, f32[32,6,1]{2,0,1:T(8,128)S(1)}, u32[]{:S(2)}, u32[]{:S(2)}) collective-permute-start(f32[32,6,1]{2,0,1:T(8,128)S(1)} %get-tuple-element.72), channel_id=1, source_target_pairs={{1,0},{2,1},{3,2},{4,3},{5,4},{6,5},{7,6},{9,8},{10,9},{11,10},{12... | collective-permute-start | bytes 2312 | tf_op jit(solution)/shard_map/ppermute | solution.py:31
  455.8 6.3 %collective-permute-start.23 = (f32[32,6,1]{2,0,1:T(8,128)S(1)}, f32[32,6,1]{2,0,1:T(8,128)S(1)}, u32[]{:S(2)}, u32[]{:S(2)}) collective-permute-start(f32[32,6,1]{2,0,1:T(8,128)S(1)} %get-tuple-element.73), channel_id=1, source_target_pairs={{0,1},{1,2},{2,3},{3,4},{4,5},{5,6},{6,7},{8,9},{9,10},{10,11},{11... | collective-permute-start | bytes 2312 | tf_op jit(solution)/shard_map/ppermute | solution.py:30
  462.2 3.1 copy-start.17
  462.6 110.8 %copy-start.19 = (f32[32,4,128]{2,1,0:T(4,128)S(1)}, f32[32,4,128]{2,1,0:T(4,128)}, u32[]{:S(2)}) copy-start(f32[32,4,128]{2,1,0:T(4,128)} %param.20) | copy-start | bytes 196612
  462.6 110.8 %copy-start.21 = (f32[32,4,128]{2,1,0:T(4,128)S(1)}, f32[32,4,128]{2,1,0:T(4,128)}, u32[]{:S(2)}) copy-start(f32[32,4,128]{2,1,0:T(4,128)} %param.23) | copy-start | bytes 196612
  462.7 110.8 %copy-start.22 = (f32[32,4,128]{2,0,1:T(8,128)S(1)}, f32[32,4,128]{2,0,1:T(8,128)}, u32[]{:S(2)}) copy-start(f32[32,4,128]{2,0,1:T(8,128)} %get-tuple-element.49) | copy-start | bytes 196612
Sparse Core Ops, SparseCore 0:
  11.4 84.1 all-gather.2
  133.3 110.2 reduce-scatter.6
  246.3 39.8 reduce-scatter.4
  289.8 86.1 all-gather.4
  416.7 32.5 reduce-scatter.8
  453.8 119.5 reduce-scatter.10

commit v2 on v1

v2 whole, which is shorter than its diff:
```python
import functools
import jax
import jax.numpy as jnp
from jax import lax
from jax.experimental import pallas as pl
from jax.experimental.pallas import tpu as pltpu
from jax.sharding import PartitionSpec as P

STEPS = 2
START = 20


BETA_ONE = 0.9
BETA_TWO = 0.99
LEARN_RATE = 0.01
EPSILON = 1e-08
NX = 16
F32 = jnp.float32
BF = jnp.bfloat16
MESH = pl.DeviceIdType.MESH


def grad_block(zb, s, tgt, xy, xz, yz, w1, w2, wo, bh, wv, b0, accxy, gxz, gyz, fbuf, dbuf, rbuf):
    wide = NX * 128
    xt = jnp.transpose(xz[s, zb])
    h1 = xt.astype(BF)
    r1 = xt - h1.astype(F32)
    h2 = r1.astype(BF)
    h3 = (r1 - h2.astype(F32)).astype(BF)
    parts = jnp.concatenate([h1, h2, h3], axis=1)
    place = lax.broadcasted_iota(jnp.int32, (3 * NX, 128), 0) % NX
    yzt = yz[s, pl.ds(zb * 8, 8)].reshape(256, 128)
    for x in range(NX):
        col = jnp.dot(parts, (place == x).astype(BF), preferred_element_type=F32)
        f = ((col * yzt).reshape(8, 32, 128) * xy[x + 1][None]).reshape(256, 128)
        fbuf[:, x * 128 : (x + 1) * 128] = f
    pre = jnp.dot(w1[...], fbuf[...].astype(BF), preferred_element_type=F32)
    q = pre.reshape(8, 32, wide) + jnp.concatenate([bh[...]] * NX, axis=-1)[None]
    u = 1.0 + jnp.tanh(q)
    h = q * u
    dbuf[...] = (u + h * (2.0 - u)) * jnp.concatenate([wv[...]] * NX, axis=-1)[None]
    out = jnp.dot(wo[...], h.reshape(256, wide).astype(BF), preferred_element_type=F32)[:8]
    for x in range(NX):
        rbuf[:, x * 128 : (x + 1) * 128] = (
            out[:, x * 128 : (x + 1) * 128] + b0 - tgt[x, pl.ds(zb * 8, 8), :]
        )
    d = (dbuf[...] * rbuf[...][:, None, :]).reshape(256, wide)
    s = jnp.dot(w2[...], d.astype(BF), preferred_element_type=F32) * fbuf[...]
    acc = None
    for x in range(NX):
        sx = s[:, x * 128 : (x + 1) * 128]
        acc = sx if acc is None else acc + sx
        accxy[x] += jnp.sum(sx.reshape(8, 32, 128), axis=0)
        gxz[zb, x : x + 1, :] = jnp.sum(sx, axis=-1).reshape(1, 256)
    gyz[pl.ds(zb * 8, 8)] = acc.reshape(8, 32, 128)


def weights(w_hidden, b_hidden, w_output):
    eye = jnp.eye(8, dtype=F32)
    wf = w_hidden.astype(F32)
    w1 = jnp.kron(eye, 0.5 * wf.T).astype(BF)
    w2 = jnp.kron(eye, wf).astype(BF)
    wof = w_output.astype(F32)
    wo = jnp.pad(jnp.kron(eye, wof[None, :]), ((0, 8), (0, 0))).astype(BF)
    bh = jnp.broadcast_to((0.5 * b_hidden)[:, None], (32, 128))
    wv = jnp.broadcast_to((0.5 * wof)[:, None], (32, 128))
    return w1, w2, wo, bh, wv


def copy_to(src, dst, send, recv, device):
    return pltpu.make_async_remote_copy(
        src_ref=src,
        dst_ref=dst,
        send_sem=send,
        recv_sem=recv,
        device_id=device,
        device_id_type=MESH,
    )


def adam(plane, first, second, grads, scale_one, scale_two):
    first = BETA_ONE * first + (1.0 - BETA_ONE) * grads
    second = BETA_TWO * second + (1.0 - BETA_TWO) * grads * grads
    plane = plane - LEARN_RATE * (first * scale_one) / (jnp.sqrt(second * scale_two) + EPSILON)
    return (plane, first, second)


def fit_kernel(
    nk,
    nj,
    tgt, xy_in, xz_in, yz_in, mxy_in, mxz_in, myz_in, vxy_in, vxz_in, vyz_in,
    w1, w2, wo, bh, wv, bo,
    xy, xz, yz, mxy, mxz, myz, vxy, vxz, vyz,
    xyp, xza, yza, gxy, gxz, gyz, sib, total, parts, xparts, fbuf, dbuf, rbuf,
    row_out, row_in, col_out, col_in,
    yz_recv, yz_send, relay_send, xz_recv, xz_send, row_recv, row_send, col_recv, col_send,
    sib_recv, sib_send, part_recv, part_send, xpart_recv, xpart_send,
):
    i = lax.axis_index("gx")
    j = lax.axis_index("gy")
    k = i // 2
    core = i % 2
    other = 1 - core
    own = nk // nj
    sibling = (2 * k + other, j)
    b0 = bo[0]
    lane = lax.broadcasted_iota(jnp.int32, (32, 128), 1)

    def chip(offset):
        return (k + offset + nk) % nk

    barrier = pltpu.get_barrier_semaphore()

    def greet(device):
        pl.semaphore_signal(barrier, inc=1, device_id=device, device_id_type=MESH)

    def greet_chip(r, carry):
        greet((2 * chip(r) + core, j))
        return carry

    def greet_column(r, carry):
        greet((i, (j + r) % nj))
        return carry

    greet(sibling)
    greet((2 * chip(1) + other, j))
    greet((2 * chip(-1) + other, j))
    lax.fori_loop(1, nk, greet_chip, 0)
    lax.fori_loop(1, nj, greet_column, 0)

    xyp[pl.ds(1, NX)] = xy_in[...]
    xza[0, pl.ds(j * own, own)] = xz_in[...]
    yza[0, pl.ds(4 * i, 4)] = yz_in[...]
    mxy[...] = mxy_in[...]
    mxz[...] = mxz_in[...]
    myz[...] = myz_in[...]
    vxy[...] = vxy_in[...]
    vxz[...] = vxz_in[...]
    vyz[...] = vyz_in[...]
    pl.semaphore_wait(barrier, nk + nj + 1)

    def yz_copy(s, r, device, slot):
        mine = yza.at[s, pl.ds(4 * i, 4)]
        return copy_to(mine, mine, yz_send.at[slot], yz_recv.at[s, k, core], device)

    def yz_wait(s, chip_index, half):
        part = yza.at[s, pl.ds(8 * chip_index + 4 * half, 4)]
        copy_to(part, part, yz_send.at[0], yz_recv.at[s, chip_index, half], sibling).wait_recv()

    def relay_copy(s, chip_index):
        part = yza.at[s, pl.ds(8 * chip_index + 4 * core, 4)]
        return copy_to(
            part, part, relay_send.at[chip_index], yz_recv.at[s, chip_index, core], sibling
        )

    def xz_copy(s, r):
        mine = xza.at[s, pl.ds(j * own, own)]
        return copy_to(mine, mine, xz_send.at[r], xz_recv.at[s, j], (i, (j + r) % nj))

    def xz_wait(s, r):
        peer = (j + r) % nj
        part = xza.at[s, pl.ds(peer * own, own)]
        copy_to(part, part, xz_send.at[0], xz_recv.at[s, peer], (i, peer)).wait_recv()

    def row_copy(s, side):
        device = ((i + 1) % (2 * nk), j) if side == 0 else ((i + 2 * nk - 1) % (2 * nk), j)
        return copy_to(
            row_out.at[side], row_in.at[s, side], row_send.at[side], row_recv.at[s, side], device
        )

    def col_copy(s, side):
        device = (i, (j + 1) % nj) if side == 0 else (i, (j + nj - 1) % nj)
        return copy_to(
            col_out.at[side], col_in.at[s, side], col_send.at[side], col_recv.at[s, side], device
        )

    def sib_copy(s, chip_index):
        return copy_to(
            gyz.at[pl.ds(8 * chip_index + 4 * other, 4)],
            sib.at[s, chip_index],
            sib_send.at[chip_index],
            sib_recv.at[s, chip_index],
            sibling,
        )

    def part_copy(s, chip_index):
        return copy_to(
            total.at[chip_index],
            parts.at[s, k],
            part_send.at[chip_index],
            part_recv.at[s, k],
            (2 * chip_index + core, j),
        )

    def part_wait(s, r):
        peer = chip(r)
        slot = parts.at[s, peer]
        copy_to(
            slot, slot, part_send.at[0], part_recv.at[s, peer], (2 * peer + core, j)
        ).wait_recv()

    def xpart_copy(s, zb):
        return copy_to(
            gxz.at[zb],
            xparts.at[s, j, zb % own],
            xpart_send.at[zb],
            xpart_recv.at[s, j, zb % own],
            (i, zb // own),
        )

    def xpart_wait(s, peer, n):
        slot = xparts.at[s, peer, n]
        copy_to(
            slot, slot, xpart_send.at[0], xpart_recv.at[s, peer, n], (i, peer)
        ).wait_recv()

    def loop(low, high, body):
        def step(r, carry):
            body(r)
            return carry

        lax.fori_loop(low, high, step, 0)

    def send_yz(s):
        yz_copy(s, 0, sibling, 0).start()
        yz_copy(s, 1, (2 * chip(-1) + core, j), 1).start()
        yz_copy(s, 1, (2 * chip(-1) + other, j), nk).start()
        loop(2, nk, lambda r: yz_copy(s, r, (2 * chip(-r) + core, j), r).start())

    def send_xz(s):
        loop(1, nj, lambda r: xz_copy(s, r).start())

    def send_borders(s):
        for side, x in ((0, NX - 1), (1, 0)):
            row_out[side, pl.ds(0, 32)] = xyp[x + 1]
            line = xza[s, pl.ds(j * own, own), x, :]
            row_out[side, pl.ds(32, own)] = line[:, :128]
            row_out[side, pl.ds(32 + own, own)] = line[:, 128:]
            row_copy(s, side).start()
        for side, last in ((0, 127), (1, 0)):
            cols = jnp.zeros((32, 128), F32)
            for n in range(NX + 4):
                piece = xyp[n + 1] if n < NX else yza[s, 4 * i + n - NX]
                cols = jnp.where(lane == n, pltpu.roll(piece, (n - last + 128) % 128, 1), cols)
            col_out[side] = cols
            col_copy(s, side).start()

    def finish_block(s, t):
        kp = chip(t)
        copy_to(
            sib.at[s, kp], sib.at[s, kp], sib_send.at[0], sib_recv.at[s, kp], sibling
        ).wait_recv()
        both = gyz[pl.ds(8 * kp + 4 * core, 4)] + sib[s, kp]

        @pl.when(t == 0)
        def _():
            parts[s, k] = both

        @pl.when(t > 0)
        def _():
            total[kp] = both
            part_copy(s, kp).start()

    def one_step(s):
        gxy[...] = jnp.zeros_like(gxy)
        loop(1, nj, lambda r: xz_wait(s, r))

        def block(t):
            kk = chip(t)
            yz_wait(s, kk, other)

            @pl.when(t == 1)
            def _():
                yz_wait(s, kk, core)

            grad_block(
                kk, s, tgt, xyp, xza, yza, w1, w2, wo, bh, wv, b0, gxy, gxz, gyz, fbuf, dbuf, rbuf
            )
            sib_copy(s, kk).start()
            keep = kk // own == j

            @pl.when(keep)
            def _():
                xparts[s, j, kk % own] = gxz[kk]

            @pl.when(jnp.logical_not(keep))
            def _():
                xpart_copy(s, kk).start()

            @pl.when(t + 2 < nk)
            def _():
                ahead = chip(t + 2)
                yz_wait(s, ahead, core)
                relay_copy(s, ahead).start()

            @pl.when(t >= 1)
            def _():
                finish_block(s, t - 1)

        loop(0, nk, block)
        finish_block(s, nk - 1)

        scale_one = jnp.where(s == 0, *(1.0 / (1.0 - BETA_ONE ** (START + n)) for n in (1, 2)))
        scale_two = jnp.where(s == 0, *(1.0 / (1.0 - BETA_TWO ** (START + n)) for n in (1, 2)))

        for side in range(2):
            row_copy(s, side).wait_recv()
            col_copy(s, side).wait_recv()
        xyp[0] = jnp.where(i == 0, xyp[1], row_in[s, 0, pl.ds(0, 32)])
        xyp[NX + 1] = jnp.where(i == 2 * nk - 1, xyp[NX], row_in[s, 1, pl.ds(0, 32)])
        before = col_in[s, 0]
        after = col_in[s, 1]

        def sides(plane, n):
            left = jnp.where(j == 0, plane, pltpu.roll(before, 128 - n, 1))
            left = jnp.where(lane == 0, left, pltpu.roll(plane, 1, 1))
            right = jnp.where(j == nj - 1, plane, pltpu.roll(after, 127 - n, 1))
            right = jnp.where(lane == 127, right, pltpu.roll(plane, 127, 1))
            return left + right

        def update_xy(x):
            plane = xyp[x + 1]
            rough = 4.0 * plane - xyp[x] - xyp[x + 2] - sides(plane, x)
            grads = gxy[x] / plane + rough
            xy[x], mxy[x], vxy[x] = adam(plane, mxy[x], vxy[x], grads, scale_one, scale_two)

        loop(0, NX, update_xy)

        for r in range(1, nj):
            for n in range(own):
                xpart_wait(s, (j + r) % nj, n)
        lane_xz = lax.broadcasted_iota(jnp.int32, (NX, 256), 1)
        spot_xz = lax.broadcasted_iota(jnp.int32, (NX, 256), 0)
        for n in range(own):
            zb = j * own + n
            plane = xza[s, zb]
            line = [
                jnp.concatenate(
                    [row_in[s, side, 32 + n : 33 + n], row_in[s, side, 32 + own + n : 33 + own + n]],
                    axis=1,
                )
                for side in range(2)
            ]
            up = jnp.where(i == 0, plane, jnp.broadcast_to(line[0], plane.shape))
            up = jnp.where(spot_xz == 0, up, pltpu.roll(plane, 1, 0))
            down = jnp.where(i == 2 * nk - 1, plane, jnp.broadcast_to(line[1], plane.shape))
            down = jnp.where(spot_xz == NX - 1, down, pltpu.roll(plane, NX - 1, 0))
            low = pltpu.roll(xza[s, jnp.maximum(zb - 1, 0)], 32, 1)
            low = jnp.where(zb == 0, plane, low)
            low = jnp.where(lane_xz < 32, low, pltpu.roll(plane, 32, 1))
            high = pltpu.roll(xza[s, jnp.minimum(zb + 1, nk - 1)], 224, 1)
            high = jnp.where(zb == nk - 1, plane, high)
            high = jnp.where(lane_xz >= 224, high, pltpu.roll(plane, 224, 1))
            term = xparts[s, 0, n]
            for peer in range(1, nj):
                term = term + xparts[s, peer, n]
            grads = term / plane + (4.0 * plane - up - down - low - high)
            xz[n], mxz[n], vxz[n] = adam(plane, mxz[n], vxz[n], grads, scale_one, scale_two)

        @pl.when(s + 1 < STEPS)
        def _():
            xza[1, pl.ds(j * own, own)] = xz[...]
            send_later(loop_xz_sent, send_xz)

        loop(1, nk, lambda r: part_wait(s, r))
        for n in range(4):
            z = 4 * i + n
            plane = yza[s, z]
            low = yza[s, jnp.maximum(z - 1, 0)]
            high = yza[s, jnp.minimum(z + 1, 8 * nk - 1)]
            rough = 4.0 * plane - low - high - sides(plane, NX + n)
            term = parts[s, 0, n]
            for peer in range(1, nk):
                term = term + parts[s, peer, n]
            grads = term / plane + rough
            yz[n], myz[n], vyz[n] = adam(plane, myz[n], vyz[n], grads, scale_one, scale_two)

        @pl.when(s + 1 < STEPS)
        def _():
            yza[1, pl.ds(4 * i, 4)] = yz[...]
            loop_yz_sent()
            send_yz(1)
            xyp[pl.ds(1, NX)] = xy[...]

        sent()

        @pl.when(s + 1 < STEPS)
        def _():
            send_borders(1)

    def loop_yz_sent():
        for slot in range(nk + 1):
            yz_copy(0, 0, sibling, slot).wait_send()

    def loop_xz_sent():
        loop(1, nj, lambda r: xz_copy(0, r).wait_send())

    def send_later(first, then):
        first()
        then(1)

    def sent():
        for side in range(2):
            row_copy(0, side).wait_send()
            col_copy(0, side).wait_send()
        loop(2, nk, lambda t: relay_copy(0, chip(t)).wait_send())
        loop(0, nk, lambda t: sib_copy(0, chip(t)).wait_send())
        loop(1, nk, lambda t: part_copy(0, chip(t)).wait_send())

        def xpart_sent(zb):
            @pl.when(zb // own != j)
            def _():
                xpart_copy(0, zb).wait_send()

        loop(0, nk, xpart_sent)

    send_yz(0)
    send_xz(0)
    send_borders(0)
    loop(0, STEPS, one_step)
    loop_yz_sent()
    loop_xz_sent()


def per_device(
    nk,
    nj,
    target,
    plane_xy,
    plane_xz,
    plane_yz,
    first_xy,
    first_xz,
    first_yz,
    second_xy,
    second_xz,
    second_yz,
    w_hidden,
    b_hidden,
    w_output,
    b_output,
):
    own = nk // nj

    def swap(a):
        return jnp.transpose(a, (1, 0, 2))

    def pack(a):
        return jnp.transpose(a.reshape(32, NX, own, 8), (2, 1, 3, 0)).reshape(own, NX, 256)

    def unpack(a):
        return jnp.transpose(a.reshape(own, NX, 8, 32), (3, 1, 0, 2)).reshape(32, NX, own * 8)

    vm = pl.BlockSpec(memory_space=pltpu.VMEM)
    shapes = [(NX, 32, 128), (own, NX, 256), (4, 32, 128)] * 3
    dma = pltpu.SemaphoreType.DMA
    outs = pl.pallas_call(
        functools.partial(fit_kernel, nk, nj),
        out_shape=[jax.ShapeDtypeStruct(shape, F32) for shape in shapes],
        in_specs=[vm] * 15 + [pl.BlockSpec(memory_space=pltpu.SMEM)],
        out_specs=[vm] * 9,
        scratch_shapes=[
            pltpu.VMEM((NX + 2, 32, 128), F32),
            pltpu.VMEM((2, nk, NX, 256), F32),
            pltpu.VMEM((2, 8 * nk, 32, 128), F32),
            pltpu.VMEM((NX, 32, 128), F32),
            pltpu.VMEM((nk, NX, 256), F32),
            pltpu.VMEM((8 * nk, 32, 128), F32),
            pltpu.VMEM((2, nk, 4, 32, 128), F32),
            pltpu.VMEM((nk, 4, 32, 128), F32),
            pltpu.VMEM((2, nk, 4, 32, 128), F32),
            pltpu.VMEM((2, nj, own, NX, 256), F32),
            pltpu.VMEM((256, NX * 128), F32),
            pltpu.VMEM((8, 32, NX * 128), F32),
            pltpu.VMEM((8, NX * 128), F32),
            pltpu.VMEM((2, 40, 128), F32),
            pltpu.VMEM((2, 2, 40, 128), F32),
            pltpu.VMEM((2, 32, 128), F32),
            pltpu.VMEM((2, 2, 32, 128), F32),
            dma((2, nk, 2)),
            dma((nk + 1,)),
            dma((nk,)),
            dma((2, nj)),
            dma((nj,)),
            dma((2, 2)),
            dma((2,)),
            dma((2, 2)),
            dma((2,)),
            dma((2, nk)),
            dma((nk,)),
            dma((2, nk)),
            dma((nk,)),
            dma((2, nj, own)),
            dma((nk,)),
        ],
        compiler_params=pltpu.CompilerParams(
            collective_id=0, has_side_effects=True, vmem_limit_bytes=56 * 2**20
        ),
    )(
        target,
        swap(plane_xy),
        pack(plane_xz),
        swap(plane_yz),
        swap(first_xy),
        pack(first_xz),
        swap(first_yz),
        swap(second_xy),
        pack(second_xz),
        swap(second_yz),
        *weights(w_hidden, b_hidden, w_output),
        b_output,
    )
    return tuple(unpack(a) if n % 3 == 1 else swap(a) for n, a in enumerate(outs))


def solution(mesh):
    piece = P(None, "gx", "gy")
    return jax.shard_map(
        functools.partial(per_device, mesh.shape["gx"] // 2, mesh.shape["gy"]),
        mesh=mesh,
        in_specs=(P("gx", None, "gy"),) + (piece,) * 9 + (P(),) * 4,
        out_specs=(piece,) * 9,
        check_vma=False,
    )
```

time: 589 us -> 153 us (0.26)
  waiting for transfers between devices: 325 us -> 0 us
  starting transfers between devices: 72.9 us -> 0 us
  Pallas kernels: 71.2 us -> 130 us
  blocking collectives: 54.3 us -> 0 us
  other arithmetic: 17.9 us -> 0.31 us
  between operations: 15.7 us -> 1.5 us
  local copies, waits for them, and re-layouts: 26.2 us -> 19.8 us
    reduce_scatter x4 -> x0, waiting for transfers between devices: 198 us -> none  [the longest x2 197 us: per_device(): lax.psum_scatter(term_yz, 'gx', scatter_dimension=1, tiled=True)]
    all_gather x2 -> x0, waiting for transfers between devices: 103 us -> none  [per_device(): whole_yz = lax.all_gather(plane_yz, 'gx', axis=1, tiled=True)]
    ppermute x24 -> x0, starting transfers between devices: 72.6 us -> none  [the longest x12 46.5 us: padded_2(): before = lax.ppermute(last, axis, up)]
    pallas_call x2 -> x1, Pallas kernels: 71.2 us -> 130 us  [per_device(): pl.pallas_call(functools.partial(fit_kernel, nk, nj), out_shape=[jax.Shap...]
    all_gather x2 -> x0, blocking collectives: 54.3 us -> none  [per_device(): whole_xz = lax.all_gather(plane_xz, 'gy', axis=2, tiled=True)]
    ppermute x24 -> x0, waiting for transfers between devices: 23.8 us -> none  [the longest x12 17.6 us: padded_2(): after = lax.ppermute(first, axis, down)]
    sub x6 -> x0, other arithmetic: 6.94 us -> none  [adam(): plane - LEARN_RATE * (first / corr_one) / (jnp.sqrt(second / corr_two) +...]
  transfers between devices with their start and end apart: 30 -> 0, of which waited for: 15 -> 0; matrix products, arithmetic and copies ran while one was open for 5% -> 0% of each run, Pallas kernels for 0% -> 0%
where the time goes in v2:
time: 153 us; the launch traced here: 152 us
  Pallas kernels  130 us (85%)
  local copies, waits for them, and re-layouts  19.8 us (13%)
    pallas_call x1, Pallas kernels, per_device(): pl.pallas_call(functools.partial(fit_kernel, nk, nj), out_shape=[jax.Shap...  130 us
    unnamed x48, local copies, waits for them, and re-layouts  9.5 us

profile of v2, /device:TPU:1, one launch (start us, length us, event | category | flops | bytes accessed | tf_op | source)
XLA Modules:
  0.0 151.8 jit_solution(14330333191770966214)
XLA Ops:
  0.6 0.0 copy-start
  0.7 0.0 copy-start.19
  1.4 0.0 copy-done.19
  1.4 0.0 copy-start.18
  1.4 0.6 copy-done.18
  2.0 0.1 mul.92
  2.1 0.7 broadcast_in_dim.15.wv
  2.8 0.0 copy-start.17
  2.8 0.7 broadcast_in_dim.14.bh
  3.5 0.0 copy-done.17
  3.5 0.1 copy.32
  3.6 0.0 copy-start.8
  3.6 0.1 mul.89
  3.6 0.1 mul.90
  3.7 0.6 pad.5.wo
  4.3 0.1 copy-done.8
  4.4 0.6 copy.55
  5.0 0.0 copy-done
  5.1 0.0 copy-start.6
  5.1 0.7 reshape.82.xz_in
  5.8 0.2 copy-done.6
  6.0 0.0 copy-start.7
  6.0 0.7 reshape.84.mxz_in
  6.7 0.2 copy-done.7
  6.9 0.0 copy-start.12
  6.9 0.0 copy-start.13
  6.9 0.0 copy-start.1
  6.9 0.7 reshape.86.vxz_in
  7.6 0.1 copy-done.12
  7.7 0.0 copy-done.13
  7.8 0.7 copy_bitcast_fusion.9
  8.4 0.0 copy-done.1
  8.4 0.0 copy-start.4
  8.4 0.8 copy.54
  9.2 0.2 copy-done.4
  9.4 0.2 copy-done.5
  9.5 0.9 copy_bitcast_fusion
  10.5 0.3 multiply_convert_fusion
  10.8 1.0 convert_element_type.33.w2
  11.8 1.0 convert_element_type.31.w1
  12.8 130.2 %shard_map.205 = (f32[16,32,128]{2,1,0:T(8,128)}, f32[2,16,256]{2,1,0:T(8,128)}, f32[4,32,128]{2,1,0:T(8,128)}, f32[16,32,128]{2,1,0:T(8,128)}, f32[2,16,256]{2,...) custom-call(f32[16,128,128]{2,1,0:T(8,128)} %tgt.1, ...), custom_call_target="tpu_custom_call" | custom-call | tf_op jit(solution)/shard_map/pallas_call | solution.py:457
  143.0 0.0 copy-start.11
  143.1 1.8 %copy.36 = f32[32,16,128]{2,1,0:T(8,128)} copy(f32[32,16,128]{2,0,1:T(8,128)} %bitcast.66) | data formatting | bytes 524288
  144.9 0.0 copy-done.11
  144.9 0.7 copy.37
  145.6 0.2 copy-done.10
  145.7 0.7 copy.39
  146.4 0.2 copy-done.9
  146.6 0.7 copy.41
  147.3 0.1 copy-done.16
  147.3 0.1 reshape.87
  147.4 0.0 copy-start.15
  147.4 0.7 copy_bitcast_fusion.5
  148.1 0.1 copy-done.15
  148.2 0.1 reshape.89
  148.3 0.0 copy-start.14
  148.3 0.7 copy_bitcast_fusion.4
  149.0 0.1 copy-done.14
  149.0 0.1 reshape.91
  149.1 0.7 copy_bitcast_fusion.3
  149.8 0.2 copy-done.3
  150.0 0.9 copy.38
  150.9 0.1 copy-done.2
  150.9 0.9 copy.40
  (16 shorter events, 0.1 us)
Async XLA Ops:
  0.6 4.4 %copy-start = (f32[32,16,16]{0,2,1:T(8,128)S(1)}, f32[32,16,16]{0,2,1:T(8,128)}, u32[]{:S(2)}) copy-start(f32[32,16,16]{0,2,1:T(8,128)} %param.16) | copy-start | bytes 98308
  0.7 0.7 copy-start.19
  1.4 0.7 copy-start.18
  2.8 0.7 copy-start.17
  3.6 0.8 copy-start.8
  5.1 0.9 copy-start.6
  6.0 0.9 copy-start.7
  6.9 0.8 copy-start.12
  6.9 0.9 copy-start.13
  6.9 1.5 copy-start.1
  8.4 1.0 copy-start.4
  8.4 1.1 copy-start.5
  143.0 1.9 %copy-start.11 = (f32[4,32,128]{2,1,0:T(8,128)S(1)}, f32[4,32,128]{2,1,0:T(8,128)}, u32[]{:S(2)}) copy-start(f32[4,32,128]{2,1,0:T(8,128)} %get-tuple-element.20) | copy-start | bytes 196612
  144.9 0.8 copy-start.10
  145.7 0.8 copy-start.9
  146.6 0.8 copy-start.16
  147.4 0.8 copy-start.15
  148.3 0.8 copy-start.14
  149.0 0.9 copy-start.3
  150.0 0.9 copy-start.2

commit v3 on v2

v3 whole, which is shorter than its diff:
```python
import functools
import jax
import jax.numpy as jnp
from jax import lax
from jax.experimental import pallas as pl
from jax.experimental.pallas import tpu as pltpu
from jax.sharding import PartitionSpec as P

STEPS = 2
START = 20


BETA_ONE = 0.9
BETA_TWO = 0.99
LEARN_RATE = 0.01
EPSILON = 1e-08
NX = 16
F32 = jnp.float32
BF = jnp.bfloat16
MESH = pl.DeviceIdType.MESH


def grad_block(
    u, low_chip, high_chip, s, tgt, xy, xz, yz, w1, w2, wo, bh, wv, b0, gxy, gxz, gyz, fbuf, dbuf, rbuf
):
    wide = NX * 128
    xt = jnp.transpose(
        jnp.concatenate([xz[s, low_chip][:, :128], xz[s, high_chip][:, 128:]], axis=1)
    )
    h1 = xt.astype(BF)
    r1 = xt - h1.astype(F32)
    h2 = r1.astype(BF)
    h3 = (r1 - h2.astype(F32)).astype(BF)
    parts = jnp.concatenate([h1, h2, h3], axis=1)
    place = lax.broadcasted_iota(jnp.int32, (3 * NX, 128), 0) % NX
    yzt = jnp.concatenate(
        [yz[s, pl.ds(8 * low_chip, 4)], yz[s, pl.ds(8 * high_chip + 4, 4)]], axis=0
    ).reshape(256, 128)
    for x in range(NX):
        col = jnp.dot(parts, (place == x).astype(BF), preferred_element_type=F32)
        f = ((col * yzt).reshape(8, 32, 128) * xy[x + 1][None]).reshape(256, 128)
        fbuf[:, x * 128 : (x + 1) * 128] = f
    pre = jnp.dot(w1[...], fbuf[...].astype(BF), preferred_element_type=F32)
    q = pre.reshape(8, 32, wide) + jnp.concatenate([bh[...]] * NX, axis=-1)[None]
    t = 1.0 + jnp.tanh(q)
    h = q * t
    dbuf[...] = (t + h * (2.0 - t)) * jnp.concatenate([wv[...]] * NX, axis=-1)[None]
    out = jnp.dot(wo[...], h.reshape(256, wide).astype(BF), preferred_element_type=F32)[:8]
    low = lax.broadcasted_iota(jnp.int32, (8, 128), 0) < 4
    for x in range(NX):
        want = jnp.where(low, tgt[x, pl.ds(8 * low_chip, 8), :], tgt[x, pl.ds(8 * high_chip, 8), :])
        rbuf[:, x * 128 : (x + 1) * 128] = out[:, x * 128 : (x + 1) * 128] + b0 - want
    d = (dbuf[...] * rbuf[...][:, None, :]).reshape(256, wide)
    p = jnp.dot(w2[...], d.astype(BF), preferred_element_type=F32) * fbuf[...]
    acc = None
    for x in range(NX):
        px = p[:, x * 128 : (x + 1) * 128]
        acc = px if acc is None else acc + px
        gxy[x] += jnp.sum(px.reshape(8, 32, 128), axis=0)
        row = jnp.sum(px, axis=-1).reshape(1, 256)
        gxz[low_chip, 0, x : x + 1, :] = row[:, :128]
        gxz[high_chip, 1, x : x + 1, :] = row[:, 128:]
    gyz[u] = acc.reshape(2, 4, 32, 128)


def copy_to(src, dst, send, recv, device):
    return pltpu.make_async_remote_copy(
        src_ref=src,
        dst_ref=dst,
        send_sem=send,
        recv_sem=recv,
        device_id=device,
        device_id_type=MESH,
    )


def adam(plane, first, second, grads, scale_one, scale_two):
    first = BETA_ONE * first + (1.0 - BETA_ONE) * grads
    second = BETA_TWO * second + (1.0 - BETA_TWO) * grads * grads
    plane = plane - LEARN_RATE * (first * scale_one) / (jnp.sqrt(second * scale_two) + EPSILON)
    return (plane, first, second)


def scales(step):
    return (1.0 / (1.0 - BETA_ONE ** (START + 1 + step)), 1.0 / (1.0 - BETA_TWO ** (START + 1 + step)))


def fit_kernel(
    nk,
    nj,
    tgt, xy_in, xz_in, yz_in, mxy_in, mxz_in, myz_in, vxy_in, vxz_in, vyz_in, w_hidden, small,
    xy_out, mxy_out, vxy_out, gxy_out, yz_out, myz_out, vyz_out, gyz_out, xz_out, mxz_out, vxz_out, gxz_out,
    xyp, mxy, vxy, mxz, vxz, gradxz, myz, vyz, xza, yza, gxy, gxz, gyz, sib, total, chain, saved, ypart, xparts,
    fbuf, dbuf, rbuf, row_out, row_in, col_out, col_in, w1, w2, wo, bh, wv,
    load, store,
    yz_recv, yz_send, relay_send, pass_send, xz_recv, xz_send, row_recv, row_send, col_recv, col_send,
    sib_recv, sib_send, chain_recv, chain_send, ypart_recv, ypart_send, xpart_recv, xpart_send,
):
    i = lax.axis_index("gx")
    j = lax.axis_index("gy")
    nz = nk // 2
    tiles = 2 * nz
    k = i // 2
    core = i % 2
    other = 1 - core
    high = k // nz
    zc = k % nz
    toward = 1 - 2 * core
    own = nk // nj
    sibling = (2 * k + other, j)
    following = (2 * (high * nz + (zc + toward + nz) % nz) + core, j)
    preceding = (2 * (high * nz + (zc - toward + nz) % nz) + core, j)
    partner = (2 * ((1 - high) * nz + zc) + core, j)
    partner_other = (2 * ((1 - high) * nz + zc) + other, j)

    def near(plane, offset, c):
        return (2 * (plane * nz + (zc + offset + nz) % nz) + c, j)

    after_row = ((i + 1) % (2 * nk), j)
    before_row = ((i + 2 * nk - 1) % (2 * nk), j)
    border = (2 * ((k + toward * (-1) + nk) % nk) + other, j)
    b0 = small[:, 64:65]
    b_hidden = small[:, :32]
    w_output = small[:, 32:64]
    lane = lax.broadcasted_iota(jnp.int32, (32, 128), 1)

    def loop(low, top, body):
        def step(r, carry):
            body(r)
            return carry

        lax.fori_loop(low, top, step, 0)

    def load_rows(src, dst, first, count, n):
        loop(0, count, lambda r: pltpu.make_async_copy(src.at[:, r, :], dst.at[first + r], load.at[n]).start())

    def loaded(dst, first, count, n):
        whole = dst.at[pl.ds(first, count)]
        pltpu.make_async_copy(whole, whole, load.at[n]).wait()

    def store_rows(src, first, dst, count, n):
        loop(0, count, lambda r: pltpu.make_async_copy(src.at[first + r], dst.at[:, r, :], store.at[n]).start())

    def stored(src, first, count, n):
        whole = src.at[pl.ds(first, count)]
        pltpu.make_async_copy(whole, whole, store.at[n]).wait()

    mine_yz = yza.at[0, pl.ds(4 * i, 4)]
    loop(0, 4, lambda r: pltpu.make_async_copy(yz_in.at[:, r, :], yza.at[0, 4 * i + r], load.at[1]).start())
    load_rows(xy_in, xyp, 1, NX, 0)
    load_rows(mxy_in, mxy, 0, NX, 2)
    load_rows(vxy_in, vxy, 0, NX, 3)
    load_rows(myz_in, myz, 0, 4, 4)
    load_rows(vyz_in, vyz, 0, 4, 5)

    barrier = pltpu.get_barrier_semaphore()

    def greet(device):
        pl.semaphore_signal(barrier, inc=1, device_id=device, device_id_type=MESH)

    targets = [sibling, partner, partner_other]
    for plane in (high, 1 - high):
        for c in (core, other):
            targets.append(near(plane, toward, c))
    for device in targets:
        greet(device)
    for device in (near(high, -toward, core), near(1 - high, -toward, core), border):
        greet(device)
    loop(1, nj, lambda r: greet((i, (j + r) % nj)))

    def gathered(src, n):
        return jnp.concatenate([src[:, 8 * n + z, :] for z in range(8)], axis=1)

    def spread(dst, n, values):
        for z in range(8):
            dst[:, 8 * n + z, :] = values[:, 32 * z : 32 * z + 32]

    for n in range(own):
        xza[0, j * own + n] = gathered(xz_in, n)
        mxz[n] = gathered(mxz_in, n)
        vxz[n] = gathered(vxz_in, n)

    def tile(u):
        t = (u // 2 + 1) % nz
        e = (u % 2 + jnp.where(t == 0, 1, 0)) % 2
        base = ((high + e) % 2) * nz
        return t, e, base + (zc - t + nz) % nz, base + (zc + t) % nz

    def my_chip(u):
        _, _, low_chip, high_chip = tile(u)
        return jnp.where(core == 0, low_chip, high_chip)

    def other_chip(u):
        _, _, low_chip, high_chip = tile(u)
        return jnp.where(core == 0, high_chip, low_chip)

    def yz_copy(s, device, slot):
        mine = yza.at[s, pl.ds(4 * i, 4)]
        return copy_to(mine, mine, yz_send.at[slot], yz_recv.at[s, k, core], device)

    def yz_wait(s, chip, half):
        part = yza.at[s, pl.ds(8 * chip + 4 * half, 4)]
        copy_to(part, part, yz_send.at[0], yz_recv.at[s, chip, half], sibling).wait_recv()

    def relay_copy(s, u):
        chip = my_chip(u)
        part = yza.at[s, pl.ds(8 * chip + 4 * core, 4)]
        return copy_to(part, part, relay_send.at[u], yz_recv.at[s, chip, core], sibling)

    def pass_copy(s, u):
        chip = my_chip(u)
        part = yza.at[s, pl.ds(8 * chip + 4 * core, 4)]
        return copy_to(part, part, pass_send.at[u], yz_recv.at[s, chip, core], following)

    def xz_copy(s, r):
        mine = xza.at[s, pl.ds(j * own, own)]
        return copy_to(mine, mine, xz_send.at[r], xz_recv.at[s, j], (i, (j + r) % nj))

    def xz_wait(s, r):
        peer = (j + r) % nj
        part = xza.at[s, pl.ds(peer * own, own)]
        copy_to(part, part, xz_send.at[0], xz_recv.at[s, peer], (i, peer)).wait_recv()

    def row_copy(s, side):
        return copy_to(
            row_out.at[side],
            row_in.at[s, side],
            row_send.at[side],
            row_recv.at[s, side],
            after_row if side == 0 else before_row,
        )

    def col_copy(s, side):
        device = (i, (j + 1) % nj) if side == 0 else (i, (j + nj - 1) % nj)
        return copy_to(
            col_out.at[side], col_in.at[s, side], col_send.at[side], col_recv.at[s, side], device
        )

    def sib_copy(s, u):
        return copy_to(gyz.at[u, other], sib.at[s, u], sib_send.at[u], sib_recv.at[s, u], sibling)

    def chain_copy(s, u, slot):
        return copy_to(
            total.at[u], chain.at[s, slot], chain_send.at[u], chain_recv.at[s, slot], following
        )

    def chain_wait(s, slot):
        part = chain.at[s, slot]
        copy_to(part, part, chain_send.at[0], chain_recv.at[s, slot], following).wait_recv()

    def ypart_copy(s):
        return copy_to(saved.at[1], ypart.at[s], ypart_send, ypart_recv.at[s], partner)

    def xpart_copy(s, chip, half):
        slot = 2 * (chip % own) + half
        return copy_to(
            gxz.at[chip, half],
            xparts.at[s, j, slot],
            xpart_send.at[chip, half],
            xpart_recv.at[s, j, slot],
            (i, chip // own),
        )

    def xpart_wait(s, peer, n):
        slot = xparts.at[s, peer, n]
        copy_to(
            slot, slot, xpart_send.at[0, 0], xpart_recv.at[s, peer, n], (i, peer)
        ).wait_recv()

    def send_yz(s):
        for slot in (3, 4, 5, 6, 0, 1, 2):
            yz_copy(s, targets[slot], slot).start()

    def yz_sent():
        for slot in range(7):
            yz_copy(0, sibling, slot).wait_send()
        loop(0, tiles - 4, lambda u: pass_copy(0, u).wait_send())
        loop(2, tiles - 2, lambda u: relay_copy(0, u).wait_send())

    def send_xz(s):
        loop(1, nj, lambda r: xz_copy(s, r).start())

    def xz_sent():
        loop(1, nj, lambda r: xz_copy(0, r).wait_send())

    def send_borders(s):
        for side, x in ((0, NX - 1), (1, 0)):
            row_out[side, pl.ds(0, 32)] = xyp[x + 1]
            line = xza[s, pl.ds(j * own, own), x, :]
            row_out[side, pl.ds(32, own)] = line[:, :128]
            row_out[side, pl.ds(32 + own, own)] = line[:, 128:]
            row_copy(s, side).start()
        for side, last in ((0, 127), (1, 0)):
            cols = jnp.zeros((32, 128), F32)
            for n in range(NX + 4):
                piece = xyp[n + 1] if n < NX else yza[s, 4 * i + n - NX]
                cols = jnp.where(lane == n, pltpu.roll(piece, (n - last + 128) % 128, 1), cols)
            col_out[side] = cols
            col_copy(s, side).start()

    def finish_tile(s, u):
        t, e, _, _ = tile(u)
        part = sib.at[s, u]
        copy_to(part, part, sib_send.at[0], sib_recv.at[s, u], sibling).wait_recv()
        both = gyz[u, core] + sib[s, u]

        @pl.when(t == 0)
        def _():
            saved[e] = both

        @pl.when(t == 1)
        def _():
            total[u] = both

        @pl.when(t >= 2)
        def _():
            chain_wait(s, u)
            total[u] = both + chain[s, u]

        @pl.when(t > 0)
        def _():
            chain_copy(s, u, jnp.where(t == nz - 1, tiles + e, u + 2)).start()

    def sent():
        for side in range(2):
            row_copy(0, side).wait_send()
            col_copy(0, side).wait_send()
        loop(0, tiles, lambda u: sib_copy(0, u).wait_send())
        loop(0, tiles - 2, lambda u: chain_copy(0, u, u).wait_send())
        ypart_copy(0).wait_send()

        def xpart_sent(chip):
            @pl.when(chip // own != j)
            def _():
                for half in range(2):
                    xpart_copy(0, chip, half).wait_send()

        loop(0, nk, xpart_sent)

    def one_step(s):
        gxy[...] = jnp.zeros_like(gxy)
        for u in range(2):
            yz_wait(s, my_chip(u), core)

            @pl.when(u + 4 < tiles)
            def _():
                pass_copy(s, u).start()

        loop(1, nj, lambda r: xz_wait(s, r))

        def block(u):
            _, _, low_chip, high_chip = tile(u)
            yz_wait(s, other_chip(u), other)
            grad_block(
                u, low_chip, high_chip, s, tgt, xyp, xza, yza, w1, w2, wo, bh, wv, b0, gxy, gxz, gyz,
                fbuf, dbuf, rbuf,
            )
            sib_copy(s, u).start()
            for half, chip in ((0, low_chip), (1, high_chip)):
                keep = chip // own == j

                @pl.when(keep)
                def _():
                    xparts[s, j, 2 * (chip % own) + half] = gxz[chip, half]

                @pl.when(jnp.logical_not(keep))
                def _():
                    xpart_copy(s, chip, half).start()

            @pl.when(u + 4 < tiles)
            def _():
                yz_wait(s, my_chip(u + 2), core)
                relay_copy(s, u + 2).start()

            @pl.when(u + 6 < tiles)
            def _():
                pass_copy(s, u + 2).start()

            @pl.when(u == tiles - 4)
            def _():
                yz_wait(s, my_chip(tiles - 2), core)

            @pl.when(u >= 1)
            def _():
                finish_tile(s, u - 1)

        loop(0, tiles, block)

        scale_one = jnp.where(s == 0, scales(0)[0], scales(1)[0])
        scale_two = jnp.where(s == 0, scales(0)[1], scales(1)[1])

        for side in range(2):
            row_copy(s, side).wait_recv()
            col_copy(s, side).wait_recv()
        chain_wait(s, tiles + 1)
        saved[1] += chain[s, tiles + 1]
        ypart_copy(s).start()

        before = col_in[s, 0]
        after = col_in[s, 1]

        def sides(plane, n):
            left = jnp.where(j == 0, plane, pltpu.roll(before, 128 - n, 1))
            left = jnp.where(lane == 0, left, pltpu.roll(plane, 1, 1))
            right = jnp.where(j == nj - 1, plane, pltpu.roll(after, 127 - n, 1))
            right = jnp.where(lane == 127, right, pltpu.roll(plane, 127, 1))
            return left + right

        xyp[0] = jnp.where(i == 0, xyp[1], row_in[s, 0, pl.ds(0, 32)])
        xyp[NX + 1] = jnp.where(i == 2 * nk - 1, xyp[NX], row_in[s, 1, pl.ds(0, 32)])

        def update_xy(x):
            plane = xyp[x + 1]
            rough = 4.0 * plane - xyp[x] - xyp[x + 2] - sides(plane, x)
            gxy[x] = gxy[x] / plane + rough

        loop(0, NX, update_xy)

        @pl.when(s == 1)
        def _():
            store_rows(gxy, 0, gxy_out, NX, 6)

        for r in range(1, nj):
            for n in range(2 * own):
                xpart_wait(s, (j + r) % nj, n)
        lane_xz = lax.broadcasted_iota(jnp.int32, (NX, 256), 1)
        spot_xz = lax.broadcasted_iota(jnp.int32, (NX, 256), 0)
        for n in range(own):
            zb = j * own + n
            plane = xza[s, zb]
            line = [
                jnp.concatenate(
                    [row_in[s, side, 32 + n : 33 + n], row_in[s, side, 32 + own + n : 33 + own + n]],
                    axis=1,
                )
                for side in range(2)
            ]
            up = jnp.where(i == 0, plane, jnp.broadcast_to(line[0], plane.shape))
            up = jnp.where(spot_xz == 0, up, pltpu.roll(plane, 1, 0))
            down = jnp.where(i == 2 * nk - 1, plane, jnp.broadcast_to(line[1], plane.shape))
            down = jnp.where(spot_xz == NX - 1, down, pltpu.roll(plane, NX - 1, 0))
            left = pltpu.roll(xza[s, jnp.maximum(zb - 1, 0)], 32, 1)
            left = jnp.where(zb == 0, plane, left)
            left = jnp.where(lane_xz < 32, left, pltpu.roll(plane, 32, 1))
            right = pltpu.roll(xza[s, jnp.minimum(zb + 1, nk - 1)], 224, 1)
            right = jnp.where(zb == nk - 1, plane, right)
            right = jnp.where(lane_xz >= 224, right, pltpu.roll(plane, 224, 1))
            terms = [
                jnp.concatenate([xparts[s, peer, 2 * n], xparts[s, peer, 2 * n + 1]], axis=1)
                for peer in range(nj)
            ]
            grads = sum(terms) / plane + (4.0 * plane - up - down - left - right)
            gradxz[n] = grads

        @pl.when(s == 0)
        def _():
            for n in range(own):
                plane, mxz[n], vxz[n] = adam(
                    xza[0, j * own + n], mxz[n], vxz[n], gradxz[n], scale_one, scale_two
                )
                xza[1, j * own + n] = plane
            xz_sent()
            send_xz(1)

        def update_yz():
            finish_tile(s, tiles - 1)
            chain_wait(s, tiles)
            copy_to(ypart.at[s], ypart.at[s], ypart_send, ypart_recv.at[s], partner).wait_recv()
            for n in range(4):
                z = 4 * i + n
                plane = yza[s, z]
                left = yza[s, jnp.maximum(z - 1, 0)]
                right = yza[s, jnp.minimum(z + 1, 8 * nk - 1)]
                rough = 4.0 * plane - left - right - sides(plane, NX + n)
                saved[0, n] = (saved[0, n] + chain[s, tiles, n] + ypart[s, n]) / plane + rough

        @pl.when(s == 0)
        def _():
            loaded(myz, 0, 4, 4)
            loaded(vyz, 0, 4, 5)
            update_yz()
            for n in range(4):
                yza[1, 4 * i + n], myz[n], vyz[n] = adam(
                    yza[0, 4 * i + n], myz[n], vyz[n], saved[0, n], scale_one, scale_two
                )
            yz_sent()
            send_yz(1)
            loaded(mxy, 0, NX, 2)
            loaded(vxy, 0, NX, 3)
            def step_xy(x):
                xyp[x + 1], mxy[x], vxy[x] = adam(
                    xyp[x + 1], mxy[x], vxy[x], gxy[x], scale_one, scale_two
                )

            loop(0, NX, step_xy)
            sent()
            send_borders(1)
            loop(
                0,
                4,
                lambda r: pltpu.make_async_copy(
                    yza.at[1, 4 * i + r], yz_out.at[:, r, :], store.at[0]
                ).start(),
            )
            store_rows(myz, 0, myz_out, 4, 1)
            store_rows(vyz, 0, vyz_out, 4, 2)
            store_rows(xyp, 1, xy_out, NX, 3)
            store_rows(mxy, 0, mxy_out, NX, 4)
            store_rows(vxy, 0, vxy_out, NX, 5)

        @pl.when(s == 1)
        def _():
            for n in range(own):
                spread(xz_out, n, xza[1, j * own + n])
                spread(mxz_out, n, mxz[n])
                spread(vxz_out, n, vxz[n])
                spread(gxz_out, n, gradxz[n])
            update_yz()
            loop(
                0,
                4,
                lambda r: pltpu.make_async_copy(
                    saved.at[0, r], gyz_out.at[:, r, :], store.at[7]
                ).start(),
            )

    wide = w_hidden[...].astype(F32)
    turned = lax.dot_general(
        w_hidden[...],
        (lax.broadcasted_iota(jnp.int32, (32, 32), 0) == lax.broadcasted_iota(jnp.int32, (32, 32), 1)).astype(BF),
        (((0,), (0,)), ((), ())),
        preferred_element_type=F32,
    )
    same = (
        lax.broadcasted_iota(jnp.int32, (256, 256), 0) // 32
        == lax.broadcasted_iota(jnp.int32, (256, 256), 1) // 32
    )

    def blocks(a):
        a = jnp.concatenate([a] * 8, axis=1)
        return jnp.where(same, jnp.concatenate([a] * 8, axis=0), 0.0).astype(BF)

    w1[...] = blocks(0.5 * turned)
    w2[...] = blocks(wide)
    line_out = jnp.broadcast_to(jnp.concatenate([w_output] * 8, axis=1), (16, 256))
    wo[...] = jnp.where(
        lax.broadcasted_iota(jnp.int32, (16, 256), 0)
        == lax.broadcasted_iota(jnp.int32, (16, 256), 1) // 32,
        line_out,
        0.0,
    ).astype(BF)
    square = lax.broadcasted_iota(jnp.int32, (32, 32), 0) == lax.broadcasted_iota(jnp.int32, (32, 32), 1)

    def column(row):
        kept = jnp.where(square, jnp.broadcast_to(row, (32, 32)), 0.0)
        return jnp.broadcast_to(jnp.sum(kept, axis=1, keepdims=True), (32, 128))

    bh[...] = column(0.5 * b_hidden)
    wv[...] = column(0.5 * w_output)

    whole = yza.at[0, pl.ds(4 * i, 4)]
    pltpu.make_async_copy(whole, whole, load.at[1]).wait()
    pl.semaphore_wait(barrier, nj + 9)
    send_yz(0)
    send_xz(0)
    loaded(xyp, 1, NX, 0)
    send_borders(0)
    loop(0, STEPS, one_step)
    sent()
    xz_sent()
    yz_sent()
    whole_one = yza.at[1, pl.ds(4 * i, 4)]
    pltpu.make_async_copy(whole_one, whole_one, store.at[0]).wait()
    stored(myz, 0, 4, 1)
    stored(vyz, 0, 4, 2)
    stored(xyp, 1, NX, 3)
    stored(mxy, 0, NX, 4)
    stored(vxy, 0, NX, 5)
    stored(gxy, 0, NX, 6)
    pltpu.make_async_copy(saved.at[0], saved.at[0], store.at[7]).wait()


def per_device(
    nk,
    nj,
    target,
    plane_xy,
    plane_xz,
    plane_yz,
    first_xy,
    first_xz,
    first_yz,
    second_xy,
    second_xz,
    second_yz,
    w_hidden,
    b_hidden,
    w_output,
    b_output,
):
    own = nk // nj

    def turn(a):
        return jnp.transpose(a, (1, 2, 0))

    vm = pl.BlockSpec(memory_space=pltpu.VMEM)
    far = pl.BlockSpec(memory_space=pl.ANY)
    dma = pltpu.SemaphoreType.DMA
    tiles = nk
    block = (4, 32, 128)
    shapes = [(32, NX, 128)] * 4 + [(32, 4, 128)] * 4 + [(NX, 8 * own, 32)] * 4
    outs = pl.pallas_call(
        functools.partial(fit_kernel, nk, nj),
        out_shape=[jax.ShapeDtypeStruct(shape, F32) for shape in shapes],
        in_specs=[vm, far, vm, far, far, vm, far, far, vm, far, vm, vm],
        out_specs=[far] * 8 + [vm] * 4,
        scratch_shapes=[
            pltpu.VMEM((NX + 2, 32, 128), F32),
            pltpu.VMEM((NX, 32, 128), F32),
            pltpu.VMEM((NX, 32, 128), F32),
            pltpu.VMEM((own, NX, 256), F32),
            pltpu.VMEM((own, NX, 256), F32),
            pltpu.VMEM((own, NX, 256), F32),
            pltpu.VMEM(block, F32),
            pltpu.VMEM(block, F32),
            pltpu.VMEM((2, nk, NX, 256), F32),
            pltpu.VMEM((2, 8 * nk, 32, 128), F32),
            pltpu.VMEM((NX, 32, 128), F32),
            pltpu.VMEM((nk, 2, NX, 128), F32),
            pltpu.VMEM((tiles, 2) + block, F32),
            pltpu.VMEM((2, tiles) + block, F32),
            pltpu.VMEM((tiles,) + block, F32),
            pltpu.VMEM((2, tiles + 2) + block, F32),
            pltpu.VMEM((2,) + block, F32),
            pltpu.VMEM((2,) + block, F32),
            pltpu.VMEM((2, nj, 2 * own, NX, 128), F32),
            pltpu.VMEM((256, NX * 128), F32),
            pltpu.VMEM((8, 32, NX * 128), F32),
            pltpu.VMEM((8, NX * 128), F32),
            pltpu.VMEM((2, 40, 128), F32),
            pltpu.VMEM((2, 2, 40, 128), F32),
            pltpu.VMEM((2, 32, 128), F32),
            pltpu.VMEM((2, 2, 32, 128), F32),
            pltpu.VMEM((256, 256), BF),
            pltpu.VMEM((256, 256), BF),
            pltpu.VMEM((16, 256), BF),
            pltpu.VMEM((32, 128), F32),
            pltpu.VMEM((32, 128), F32),
            dma((6,)),
            dma((8,)),
            dma((2, nk, 2)),
            dma((7,)),
            dma((tiles,)),
            dma((tiles,)),
            dma((2, nj)),
            dma((nj,)),
            dma((2, 2)),
            dma((2,)),
            dma((2, 2)),
            dma((2,)),
            dma((2, tiles)),
            dma((tiles,)),
            dma((2, tiles + 2)),
            dma((tiles,)),
            dma((2,)),
            dma,
            dma((2, nj, 2 * own)),
            dma((nk, 2)),
        ],
        compiler_params=pltpu.CompilerParams(
            collective_id=0, has_side_effects=True, vmem_limit_bytes=56 * 2**20
        ),
    )(
        target,
        plane_xy,
        turn(plane_xz),
        plane_yz,
        first_xy,
        turn(first_xz),
        first_yz,
        second_xy,
        turn(second_xz),
        second_yz,
        w_hidden,
        jnp.concatenate(
            [b_hidden, w_output.astype(F32), b_output, jnp.zeros((63,), F32)]
        ).reshape(1, 128),
    )
    xy, mxy, vxy, gxy, yz, myz, vyz, gyz, xz, mxz, vxz, gxz = outs
    xy, mxy, vxy = adam(xy, mxy, vxy, gxy, *scales(1))
    yz, myz, vyz = adam(yz, myz, vyz, gyz, *scales(1))
    xz, mxz, vxz = (jnp.transpose(a, (2, 0, 1)) for a in adam(xz, mxz, vxz, gxz, *scales(1)))
    return (xy, xz, yz, mxy, mxz, myz, vxy, vxz, vyz)


def solution(mesh):
    piece = P(None, "gx", "gy")
    return jax.shard_map(
        functools.partial(per_device, mesh.shape["gx"] // 2, mesh.shape["gy"]),
        mesh=mesh,
        in_specs=(P("gx", None, "gy"),) + (piece,) * 9 + (P(),) * 4,
        out_specs=(piece,) * 9,
        check_vma=False,
    )
```

time: 153 us -> 133 us (0.87)
  local copies, waits for them, and re-layouts: 19.8 us -> 0.66 us
  other arithmetic: 0.31 us -> 5.88 us
  Pallas kernels: 130 us -> 125 us
    unnamed x48 -> x12, local copies, waits for them, and re-layouts: 9.5 us -> 0.66 us
    pallas_call x1, Pallas kernels: 130 us -> 125 us  [per_device(): pl.pallas_call(functools.partial(fit_kernel, nk, nj), out_shape=[jax.Shap...]
    reshape x9 -> x0, local copies, waits for them, and re-layouts: 4.35 us -> none  [the longest x3 2.11 us: pack(): jnp.transpose(a.reshape(32, NX, own, 8), (2, 1, 3, 0)).reshape(own, NX, 256)]
    sub x0 -> x2, other arithmetic: none -> 2.7 us  [adam(): plane - LEARN_RATE * (first * scale_one) / (jnp.sqrt(second * scale_two)...]
    convert_element_type x2 -> x0, local copies, waits for them, and re-layouts: 2.04 us -> none  [the longest x1 1.02 us: weights(): w2 = jnp.kron(eye, wf).astype(BF)]
    transpose x0 -> x1, other arithmetic: none -> 1.93 us  [per_device(): jnp.transpose(a, (2, 0, 1))]
    transpose x5 -> x0, local copies, waits for them, and re-layouts: 1.63 us -> none  [the longest x2 1.6 us: swap(): return jnp.transpose(a, (1, 0, 2))]
where the time goes in v3:
time: 133 us; the launch traced here: 132 us
  Pallas kernels  125 us (94%)
  other arithmetic  5.88 us (4%)
  between operations  1.36 us (1%)
    pallas_call x1, Pallas kernels, per_device(): pl.pallas_call(functools.partial(fit_kernel, nk, nj), out_shape=[jax.Shap...  125 us
    sub x2, other arithmetic, adam(): plane - LEARN_RATE * (first * scale_one) / (jnp.sqrt(second * scale_two)...  2.7 us

profile of v3, /device:TPU:1, one launch (start us, length us, event | category | flops | bytes accessed | tf_op | source)
XLA Modules:
  0.0 132.4 jit_solution(16817113712400724047)
XLA Ops:
  0.6 0.7 convert_element_type.3
  2.0 0.0 copy-start.5
  2.0 0.6 copy-done.5
  2.6 0.6 maximum_bitcast_fusion.small
  3.2 124.5 %shard_map.205 = (f32[32,16,128]{2,1,0:T(8,128)}, f32[32,16,128]{2,1,0:T(8,128)}, f32[32,16,128]{2,1,0:T(8,128)}, f32[32,16,128]{2,1,0:T(8,128)}, f32[32,4,128]{...) custom-call(f32[16,128,128]{2,1,0:T(8,128)} %tgt.1, ...), custom_call_target="tpu_custom_call" | custom-call | tf_op jit(solution)/shard_map/pallas_call | solution.py:612
  127.8 0.0 copy-start.4
  127.8 0.0 copy-start.3
  127.8 1.7 %divide_subtract_fusion.1 = (f32[32,4,128]{2,1,0:T(4,128)}, f32[32,4,128]{2,1,0:T(4,128)}, f32[32,4,128]{2,1,0:T(4,128)}) fusion(f32[32,4,128]{2,1,0:T(4,128)} %get-tuple-element.29, f32[32,4,128]{2,1,0:T(4,128)} %get-tuple-element.31, f32[32,4,128]{2,1,0:T(4,128)} %get-tuple-element.30, f32[32,4,128]{2,1,0:T(4,128)} %get-tuple-element.32), kind=kLoop, calls=%fused_computation.10 | loop fusion | flops 196608 | bytes 458752 | tf_op jit(solution)/shard_map/sub | solution.py:80
  129.5 0.0 copy-done.4
  129.5 0.0 copy-start
  129.5 0.0 copy-start.1
  129.5 0.0 copy-start.2
  129.5 1.9 %fusion.4 = (f32[32,16,16]{0,2,1:T(8,128)}, f32[32,16,16]{0,2,1:T(8,128)}, f32[32,16,16]{0,2,1:T(8,128)}) fusion(f32[16,16,32]{2,1,0:T(8,128)} %get-tuple-element.27, f32[16,16,32]{2,1,0:T(8,128)} %get-tuple-element.28, f32[16,16,32]{2,1,0:T(8,128)S(1)} %copy-done.4, f32[16,16,32]{2,1,0:T(8,128)} %get-tuple-element.26), kind=kLoop, calls=%fused_computation.13 | loop fusion | flops 98304 | bytes 229376 | tf_op jit(solution)/shard_map/transpose | solution.py:692
  131.5 0.0 copy-done.3
  131.5 0.0 copy-done
  131.5 0.0 copy-done.1
  131.5 0.0 copy-done.2
  131.5 1.0 divide_subtract_fusion
  (1 shorter events, 0.0 us)
Async XLA Ops:
  2.0 0.7 copy-start.5
  127.8 1.8 %copy-start.4 = (f32[16,16,32]{2,1,0:T(8,128)S(1)}, f32[16,16,32]{2,1,0:T(8,128)}, u32[]{:S(2)}) copy-start(f32[16,16,32]{2,1,0:T(8,128)} %get-tuple-element.25) | copy-start | bytes 98308
  127.8 3.7 %copy-start.3 = (f32[32,16,128]{2,1,0:T(8,128)S(1)}, f32[32,16,128]{2,1,0:T(8,128)}, u32[]{:S(2)}) copy-start(f32[32,16,128]{2,1,0:T(8,128)} %get-tuple-element.23) | copy-start | bytes 786436
  129.5 1.9 %copy-start = (f32[32,16,128]{2,1,0:T(8,128)S(1)}, f32[32,16,128]{2,1,0:T(8,128)}, u32[]{:S(2)}) copy-start(f32[32,16,128]{2,1,0:T(8,128)} %get-tuple-element.21) | copy-start | bytes 786436
  129.5 2.0 %copy-start.1 = (f32[32,16,128]{2,1,0:T(8,128)S(1)}, f32[32,16,128]{2,1,0:T(8,128)}, u32[]{:S(2)}) copy-start(f32[32,16,128]{2,1,0:T(8,128)} %get-tuple-element.22) | copy-start | bytes 786436
  129.5 2.0 %copy-start.2 = (f32[32,16,128]{2,1,0:T(8,128)S(1)}, f32[32,16,128]{2,1,0:T(8,128)}, u32[]{:S(2)}) copy-start(f32[32,16,128]{2,1,0:T(8,128)} %get-tuple-element.24) | copy-start | bytes 786436

commit v4 on v3

--- a/solution.py
+++ b/solution.py
@@ -21,7 +21,7 @@
 
 
 def grad_block(
-    u, low_chip, high_chip, s, tgt, xy, xz, yz, w1, w2, wo, bh, wv, b0, gxy, gxz, gyz, fbuf, dbuf, rbuf
+    tt, side, low_chip, high_chip, low_row, high_row, s, tgt, xy, xz, yz, w1, w2, wo, bh, wv, b0, gxy, gxz, gyz, fbuf, dbuf, rbuf
 ):
     wide = NX * 128
     xt = jnp.transpose(
@@ -34,7 +34,7 @@
     parts = jnp.concatenate([h1, h2, h3], axis=1)
     place = lax.broadcasted_iota(jnp.int32, (3 * NX, 128), 0) % NX
     yzt = jnp.concatenate(
-        [yz[s, pl.ds(8 * low_chip, 4)], yz[s, pl.ds(8 * high_chip + 4, 4)]], axis=0
+        [yz[s, pl.ds(low_row, 4)], yz[s, pl.ds(high_row, 4)]], axis=0
     ).reshape(256, 128)
     for x in range(NX):
         col = jnp.dot(parts, (place == x).astype(BF), preferred_element_type=F32)
@@ -57,10 +57,22 @@
         px = p[:, x * 128 : (x + 1) * 128]
         acc = px if acc is None else acc + px
         gxy[x] += jnp.sum(px.reshape(8, 32, 128), axis=0)
-        row = jnp.sum(px, axis=-1).reshape(1, 256)
+        if x % 4 == 0:
+            top = px.astype(BF)
+            rest = (px - top.astype(F32)).astype(BF)
+            row = sum(
+                lax.dot_general(
+                    jnp.ones((16, 128), BF), part, (((1,), (1,)), ((), ())), preferred_element_type=F32
+                )[0:1]
+                for part in (top, rest)
+            )
+        else:
+            row = jnp.sum(px, axis=-1).reshape(1, 256)
         gxz[low_chip, 0, x : x + 1, :] = row[:, :128]
         gxz[high_chip, 1, x : x + 1, :] = row[:, 128:]
-    gyz[u] = acc.reshape(2, 4, 32, 128)
+    halves = acc.reshape(2, 4, 32, 128)
+    gyz[tt, 0, side] = halves[0]
+    gyz[tt, 1, side] = halves[1]
 
 
 def copy_to(src, dst, send, recv, device):
@@ -124,6 +136,15 @@
     w_output = small[:, 32:64]
     lane = lax.broadcasted_iota(jnp.int32, (32, 128), 1)
 
+    def place(plane, zz, half):
+        return 4 * ((zz * 2 + half) * 2 + plane)
+
+    def row_of(device):
+        chip = device // 2
+        return place(chip // nz, chip % nz, device % 2)
+
+    mine = row_of(i)
+
     def loop(low, top, body):
         def step(r, carry):
             body(r)
@@ -145,8 +166,7 @@
         whole = src.at[pl.ds(first, count)]
         pltpu.make_async_copy(whole, whole, store.at[n]).wait()
 
-    mine_yz = yza.at[0, pl.ds(4 * i, 4)]
-    loop(0, 4, lambda r: pltpu.make_async_copy(yz_in.at[:, r, :], yza.at[0, 4 * i + r], load.at[1]).start())
+    loop(0, 4, lambda r: pltpu.make_async_copy(yz_in.at[:, r, :], yza.at[0, mine + r], load.at[1]).start())
     load_rows(xy_in, xyp, 1, NX, 0)
     load_rows(mxy_in, mxy, 0, NX, 2)
     load_rows(vxy_in, vxy, 0, NX, 3)
@@ -180,37 +200,39 @@
         mxz[n] = gathered(mxz_in, n)
         vxz[n] = gathered(vxz_in, n)
 
-    def tile(u):
-        t = (u // 2 + 1) % nz
-        e = (u % 2 + jnp.where(t == 0, 1, 0)) % 2
-        base = ((high + e) % 2) * nz
-        return t, e, base + (zc - t + nz) % nz, base + (zc + t) % nz
-
-    def my_chip(u):
-        _, _, low_chip, high_chip = tile(u)
-        return jnp.where(core == 0, low_chip, high_chip)
-
-    def other_chip(u):
-        _, _, low_chip, high_chip = tile(u)
-        return jnp.where(core == 0, high_chip, low_chip)
+    def away(tt):
+        return (tt + 1) % nz
+
+    def my_z(tt):
+        return (zc - toward * away(tt) + nz) % nz
+
+    def other_z(tt):
+        return (zc + toward * away(tt) + nz) % nz
 
     def yz_copy(s, device, slot):
-        mine = yza.at[s, pl.ds(4 * i, 4)]
-        return copy_to(mine, mine, yz_send.at[slot], yz_recv.at[s, k, core], device)
-
-    def yz_wait(s, chip, half):
-        part = yza.at[s, pl.ds(8 * chip + 4 * half, 4)]
-        copy_to(part, part, yz_send.at[0], yz_recv.at[s, chip, half], sibling).wait_recv()
-
-    def relay_copy(s, u):
-        chip = my_chip(u)
-        part = yza.at[s, pl.ds(8 * chip + 4 * core, 4)]
-        return copy_to(part, part, relay_send.at[u], yz_recv.at[s, chip, core], sibling)
-
-    def pass_copy(s, u):
-        chip = my_chip(u)
-        part = yza.at[s, pl.ds(8 * chip + 4 * core, 4)]
-        return copy_to(part, part, pass_send.at[u], yz_recv.at[s, chip, core], following)
+        part = yza.at[s, pl.ds(mine, 4)]
+        return copy_to(part, part, yz_send.at[slot], yz_recv.at[s, zc, core, 1 + high], device)
+
+    def one_wait(s, zz, half, plane):
+        part = yza.at[s, pl.ds(place(plane, zz, half), 4)]
+        copy_to(
+            part, part, yz_send.at[0], yz_recv.at[s, zz, half, 1 + plane], sibling
+        ).wait_recv()
+
+    def pair_of(s, zz, half):
+        return yza.at[s, pl.ds(place(0, zz, half), 8)]
+
+    def pair_wait(s, zz, half):
+        part = pair_of(s, zz, half)
+        copy_to(part, part, yz_send.at[0], yz_recv.at[s, zz, half, 0], sibling).wait_recv()
+
+    def relay_copy(s, tt):
+        part = pair_of(s, my_z(tt), core)
+        return copy_to(part, part, relay_send.at[tt], yz_recv.at[s, my_z(tt), core, 0], sibling)
+
+    def pass_copy(s, tt):
+        part = pair_of(s, my_z(tt), core)
+        return copy_to(part, part, pass_send.at[tt], yz_recv.at[s, my_z(tt), core, 0], following)
 
     def xz_copy(s, r):
         mine = xza.at[s, pl.ds(j * own, own)]
@@ -236,36 +258,46 @@
             col_out.at[side], col_in.at[s, side], col_send.at[side], col_recv.at[s, side], device
         )
 
-    def sib_copy(s, u):
-        return copy_to(gyz.at[u, other], sib.at[s, u], sib_send.at[u], sib_recv.at[s, u], sibling)
-
-    def chain_copy(s, u, slot):
+    def sib_copy(s, tt):
         return copy_to(
-            total.at[u], chain.at[s, slot], chain_send.at[u], chain_recv.at[s, slot], following
+            gyz.at[tt, other], sib.at[s, tt], sib_send.at[tt], sib_recv.at[s, tt], sibling
         )
 
-    def chain_wait(s, slot):
-        part = chain.at[s, slot]
-        copy_to(part, part, chain_send.at[0], chain_recv.at[s, slot], following).wait_recv()
+    def last_copy(s, side):
+        return copy_to(
+            gyz.at[nz - 1, other, side],
+            sib.at[s, nz - 1, side],
+            sib_send.at[nz - 1 + side],
+            sib_recv.at[s, nz - 1 + side],
+            sibling,
+        )
+
+    def chain_copy(s, tt):
+        return copy_to(
+            total.at[tt], chain.at[s, tt + 1], chain_send.at[tt], chain_recv.at[s, tt + 1], following
+        )
+
+    def chain_wait(s, tt):
+        part = chain.at[s, tt]
+        copy_to(part, part, chain_send.at[0], chain_recv.at[s, tt], following).wait_recv()
 
     def ypart_copy(s):
         return copy_to(saved.at[1], ypart.at[s], ypart_send, ypart_recv.at[s], partner)
 
-    def xpart_copy(s, chip, half):
-        slot = 2 * (chip % own) + half
+    def xpart_copy(s, r):
+        peer = (j + r) % nj
         return copy_to(
-            gxz.at[chip, half],
-            xparts.at[s, j, slot],
-            xpart_send.at[chip, half],
-            xpart_recv.at[s, j, slot],
-            (i, chip // own),
+            gxz.at[pl.ds(own * peer, own)],
+            xparts.at[s, j],
+            xpart_send.at[r],
+            xpart_recv.at[s, j],
+            (i, peer),
         )
 
-    def xpart_wait(s, peer, n):
-        slot = xparts.at[s, peer, n]
-        copy_to(
-            slot, slot, xpart_send.at[0, 0], xpart_recv.at[s, peer, n], (i, peer)
-        ).wait_recv()
+    def xpart_wait(s, r):
+        peer = (j + r) % nj
+        slot = xparts.at[s, peer]
+        copy_to(slot, slot, xpart_send.at[0], xpart_recv.at[s, peer], (i, peer)).wait_recv()
 
     def send_yz(s):
         for slot in (3, 4, 5, 6, 0, 1, 2):
@@ -274,8 +306,8 @@
     def yz_sent():
         for slot in range(7):
             yz_copy(0, sibling, slot).wait_send()
-        loop(0, tiles - 4, lambda u: pass_copy(0, u).wait_send())
-        loop(2, tiles - 2, lambda u: relay_copy(0, u).wait_send())
+        loop(0, nz - 2, lambda tt: pass_copy(0, tt).wait_send())
+        loop(1, nz - 1, lambda tt: relay_copy(0, tt).wait_send())
 
     def send_xz(s):
         loop(1, nj, lambda r: xz_copy(s, r).start())
@@ -293,98 +325,94 @@
         for side, last in ((0, 127), (1, 0)):
             cols = jnp.zeros((32, 128), F32)
             for n in range(NX + 4):
-                piece = xyp[n + 1] if n < NX else yza[s, 4 * i + n - NX]
+                piece = xyp[n + 1] if n < NX else yza[s, mine + n - NX]
                 cols = jnp.where(lane == n, pltpu.roll(piece, (n - last + 128) % 128, 1), cols)
             col_out[side] = cols
             col_copy(s, side).start()
 
-    def finish_tile(s, u):
-        t, e, _, _ = tile(u)
-        part = sib.at[s, u]
-        copy_to(part, part, sib_send.at[0], sib_recv.at[s, u], sibling).wait_recv()
-        both = gyz[u, core] + sib[s, u]
-
-        @pl.when(t == 0)
+    def finish_pair(s, tt):
+        sib_copy(s, tt).wait_recv()
+
+        @pl.when(tt == 0)
         def _():
-            saved[e] = both
-
-        @pl.when(t == 1)
+            total[tt] = gyz[tt, core] + sib[s, tt]
+
+        @pl.when(tt > 0)
         def _():
-            total[u] = both
-
-        @pl.when(t >= 2)
-        def _():
-            chain_wait(s, u)
-            total[u] = both + chain[s, u]
-
-        @pl.when(t > 0)
-        def _():
-            chain_copy(s, u, jnp.where(t == nz - 1, tiles + e, u + 2)).start()
+            chain_wait(s, tt)
+            total[tt] = gyz[tt, core] + sib[s, tt] + chain[s, tt]
+
+        chain_copy(s, tt).start()
 
     def sent():
         for side in range(2):
             row_copy(0, side).wait_send()
             col_copy(0, side).wait_send()
-        loop(0, tiles, lambda u: sib_copy(0, u).wait_send())
-        loop(0, tiles - 2, lambda u: chain_copy(0, u, u).wait_send())
+        loop(0, nz - 1, lambda tt: sib_copy(0, tt).wait_send())
+        loop(0, 2, lambda side: last_copy(0, side).wait_send())
+        loop(0, nz - 1, lambda tt: chain_copy(0, tt).wait_send())
         ypart_copy(0).wait_send()
-
-        def xpart_sent(chip):
-            @pl.when(chip // own != j)
-            def _():
-                for half in range(2):
-                    xpart_copy(0, chip, half).wait_send()
-
-        loop(0, nk, xpart_sent)
+        loop(1, nj, lambda r: xpart_copy(0, r).wait_send())
 
     def one_step(s):
         gxy[...] = jnp.zeros_like(gxy)
-        for u in range(2):
-            yz_wait(s, my_chip(u), core)
-
-            @pl.when(u + 4 < tiles)
+        for plane in range(2):
+            one_wait(s, my_z(0), core, plane)
+        if nz > 2:
+            pass_copy(s, 0).start()
+        for plane in range(2):
+            one_wait(s, other_z(0), other, plane)
+
+        loop(1, nj, lambda r: xz_wait(s, r))
+
+        def block(u):
+            tt = u // 2
+            side = u % 2
+            t = away(tt)
+            plane = (high + side + jnp.where(t == 0, 1, 0)) % 2
+            low_z = (zc - t + nz) % nz
+            high_z = (zc + t) % nz
+
+            @pl.when((side == 0) & (tt > 0) & (tt < nz - 1))
             def _():
-                pass_copy(s, u).start()
-
-        loop(1, nj, lambda r: xz_wait(s, r))
-
-        def block(u):
-            _, _, low_chip, high_chip = tile(u)
-            yz_wait(s, other_chip(u), other)
+                pair_wait(s, other_z(tt), other)
+
+            @pl.when(u == tiles - 2)
+            def _():
+                one_wait(s, zc, core, 1 - high)
+                one_wait(s, zc, other, 1 - high)
+                one_wait(s, zc, other, high)
+
             grad_block(
-                u, low_chip, high_chip, s, tgt, xyp, xza, yza, w1, w2, wo, bh, wv, b0, gxy, gxz, gyz,
-                fbuf, dbuf, rbuf,
+                tt, side, plane * nz + low_z, plane * nz + high_z,
+                place(plane, low_z, 0), place(plane, high_z, 1),
+                s, tgt, xyp, xza, yza, w1, w2, wo, bh, wv, b0, gxy, gxz, gyz, fbuf, dbuf, rbuf,
             )
-            sib_copy(s, u).start()
-            for half, chip in ((0, low_chip), (1, high_chip)):
-                keep = chip // own == j
-
-                @pl.when(keep)
-                def _():
-                    xparts[s, j, 2 * (chip % own) + half] = gxz[chip, half]
-
-                @pl.when(jnp.logical_not(keep))
-                def _():
-                    xpart_copy(s, chip, half).start()
-
-            @pl.when(u + 4 < tiles)
+
+            @pl.when(tt == nz - 1)
             def _():
-                yz_wait(s, my_chip(u + 2), core)
-                relay_copy(s, u + 2).start()
-
-            @pl.when(u + 6 < tiles)
+                last_copy(s, side).start()
+
+            @pl.when((side == 1) & (tt < nz - 1))
             def _():
-                pass_copy(s, u + 2).start()
-
-            @pl.when(u == tiles - 4)
+                sib_copy(s, tt).start()
+
+            @pl.when((side == 0) & (tt + 2 < nz))
             def _():
-                yz_wait(s, my_chip(tiles - 2), core)
-
-            @pl.when(u >= 1)
+                pair_wait(s, my_z(tt + 1), core)
+                relay_copy(s, tt + 1).start()
+
+            @pl.when((side == 0) & (tt + 3 < nz))
             def _():
-                finish_tile(s, u - 1)
+                pass_copy(s, tt + 1).start()
+
+            @pl.when((side == 0) & (tt > 0))
+            def _():
+                finish_pair(s, tt - 1)
 
         loop(0, tiles, block)
+        loop(1, nj, lambda r: xpart_copy(s, r).start())
+        xparts[s, j] = gxz[pl.ds(own * j, own)]
 
         scale_one = jnp.where(s == 0, scales(0)[0], scales(1)[0])
         scale_two = jnp.where(s == 0, scales(0)[1], scales(1)[1])
@@ -392,8 +420,9 @@
         for side in range(2):
             row_copy(s, side).wait_recv()
             col_copy(s, side).wait_recv()
-        chain_wait(s, tiles + 1)
-        saved[1] += chain[s, tiles + 1]
+        chain_wait(s, nz - 1)
+        last_copy(s, 0).wait_recv()
+        saved[1] = gyz[nz - 1, core, 0] + sib[s, nz - 1, 0] + chain[s, nz - 1, 1]
         ypart_copy(s).start()
 
         before = col_in[s, 0]
@@ -420,9 +449,7 @@
         def _():
             store_rows(gxy, 0, gxy_out, NX, 6)
 
-        for r in range(1, nj):
-            for n in range(2 * own):
-                xpart_wait(s, (j + r) % nj, n)
+        loop(1, nj, lambda r: xpart_wait(s, r))
         lane_xz = lax.broadcasted_iota(jnp.int32, (NX, 256), 1)
         spot_xz = lax.broadcasted_iota(jnp.int32, (NX, 256), 0)
         for n in range(own):
@@ -446,7 +473,7 @@
             right = jnp.where(zb == nk - 1, plane, right)
             right = jnp.where(lane_xz >= 224, right, pltpu.roll(plane, 224, 1))
             terms = [
-                jnp.concatenate([xparts[s, peer, 2 * n], xparts[s, peer, 2 * n + 1]], axis=1)
+                jnp.concatenate([xparts[s, peer, n, 0], xparts[s, peer, n, 1]], axis=1)
                 for peer in range(nj)
             ]
             grads = sum(terms) / plane + (4.0 * plane - up - down - left - right)
@@ -463,16 +490,21 @@
             send_xz(1)
 
         def update_yz():
-            finish_tile(s, tiles - 1)
-            chain_wait(s, tiles)
+            last_copy(s, 1).wait_recv()
             copy_to(ypart.at[s], ypart.at[s], ypart_send, ypart_recv.at[s], partner).wait_recv()
             for n in range(4):
-                z = 4 * i + n
-                plane = yza[s, z]
-                left = yza[s, jnp.maximum(z - 1, 0)]
-                right = yza[s, jnp.minimum(z + 1, 8 * nk - 1)]
+                plane = yza[s, mine + n]
+                back = mine + n - 1 if n > 0 else jnp.where(i == 0, mine, row_of(jnp.maximum(i - 1, 0)) + 3)
+                ahead = (
+                    mine + n + 1
+                    if n < 3
+                    else jnp.where(i == 2 * nk - 1, mine + 3, row_of(jnp.minimum(i + 1, 2 * nk - 1)))
+                )
+                left = yza[s, back]
+                right = yza[s, ahead]
                 rough = 4.0 * plane - left - right - sides(plane, NX + n)
-                saved[0, n] = (saved[0, n] + chain[s, tiles, n] + ypart[s, n]) / plane + rough
+                term = gyz[nz - 1, core, 1, n] + sib[s, nz - 1, 1, n] + chain[s, nz - 1, 0, n] + ypart[s, n]
+                saved[0, n] = term / plane + rough
 
         @pl.when(s == 0)
         def _():
@@ -480,8 +512,8 @@
             loaded(vyz, 0, 4, 5)
             update_yz()
             for n in range(4):
-                yza[1, 4 * i + n], myz[n], vyz[n] = adam(
-                    yza[0, 4 * i + n], myz[n], vyz[n], saved[0, n], scale_one, scale_two
+                yza[1, mine + n], myz[n], vyz[n] = adam(
+                    yza[0, mine + n], myz[n], vyz[n], saved[0, n], scale_one, scale_two
                 )
             yz_sent()
             send_yz(1)
@@ -499,7 +531,7 @@
                 0,
                 4,
                 lambda r: pltpu.make_async_copy(
-                    yza.at[1, 4 * i + r], yz_out.at[:, r, :], store.at[0]
+                    yza.at[1, mine + r], yz_out.at[:, r, :], store.at[0]
                 ).start(),
             )
             store_rows(myz, 0, myz_out, 4, 1)
@@ -558,7 +590,7 @@
     bh[...] = column(0.5 * b_hidden)
     wv[...] = column(0.5 * w_output)
 
-    whole = yza.at[0, pl.ds(4 * i, 4)]
+    whole = yza.at[0, pl.ds(mine, 4)]
     pltpu.make_async_copy(whole, whole, load.at[1]).wait()
     pl.semaphore_wait(barrier, nj + 9)
     send_yz(0)
@@ -569,7 +601,7 @@
     sent()
     xz_sent()
     yz_sent()
-    whole_one = yza.at[1, pl.ds(4 * i, 4)]
+    whole_one = yza.at[1, pl.ds(mine, 4)]
     pltpu.make_async_copy(whole_one, whole_one, store.at[0]).wait()
     stored(myz, 0, 4, 1)
     stored(vyz, 0, 4, 2)
@@ -606,7 +638,7 @@
     vm = pl.BlockSpec(memory_space=pltpu.VMEM)
     far = pl.BlockSpec(memory_space=pl.ANY)
     dma = pltpu.SemaphoreType.DMA
-    tiles = nk
+    nz = nk // 2
     block = (4, 32, 128)
     shapes = [(32, NX, 128)] * 4 + [(32, 4, 128)] * 4 + [(NX, 8 * own, 32)] * 4
     outs = pl.pallas_call(
@@ -627,13 +659,13 @@
             pltpu.VMEM((2, 8 * nk, 32, 128), F32),
             pltpu.VMEM((NX, 32, 128), F32),
             pltpu.VMEM((nk, 2, NX, 128), F32),
-            pltpu.VMEM((tiles, 2) + block, F32),
-            pltpu.VMEM((2, tiles) + block, F32),
-            pltpu.VMEM((tiles,) + block, F32),
-            pltpu.VMEM((2, tiles + 2) + block, F32),
+            pltpu.VMEM((nz, 2, 2) + block, F32),
+            pltpu.VMEM((2, nz, 2) + block, F32),
+            pltpu.VMEM((nz, 2) + block, F32),
+            pltpu.VMEM((2, nz, 2) + block, F32),
             pltpu.VMEM((2,) + block, F32),
             pltpu.VMEM((2,) + block, F32),
-            pltpu.VMEM((2, nj, 2 * own, NX, 128), F32),
+            pltpu.VMEM((2, nj, own, 2, NX, 128), F32),
             pltpu.VMEM((256, NX * 128), F32),
             pltpu.VMEM((8, 32, NX * 128), F32),
             pltpu.VMEM((8, NX * 128), F32),
@@ -648,24 +680,24 @@
             pltpu.VMEM((32, 128), F32),
             dma((6,)),
             dma((8,)),
-            dma((2, nk, 2)),
+            dma((2, nz, 2, 3)),
             dma((7,)),
-            dma((tiles,)),
-            dma((tiles,)),
+            dma((nz,)),
+            dma((nz,)),
             dma((2, nj)),
             dma((nj,)),
             dma((2, 2)),
             dma((2,)),
             dma((2, 2)),
             dma((2,)),
-            dma((2, tiles)),
-            dma((tiles,)),
-            dma((2, tiles + 2)),
-            dma((tiles,)),
+            dma((2, nz + 1)),
+            dma((nz + 1,)),
+            dma((2, nz)),
+            dma((nz,)),
             dma((2,)),
             dma,
-            dma((2, nj, 2 * own)),
-            dma((nk, 2)),
+            dma((2, nj)),
+            dma((nj,)),
         ],
         compiler_params=pltpu.CompilerParams(
             collective_id=0, has_side_effects=True, vmem_limit_bytes=56 * 2**20

time: 133 us -> 132 us (level)
  no operation moved by 1% of the time
where the time goes in v4:
time: 132 us
  Pallas kernels  124 us (94%)
  other arithmetic  5.88 us (4%)
  between operations  1.36 us (1%)
    pallas_call x1, Pallas kernels, per_device(): pl.pallas_call(functools.partial(fit_kernel, nk, nj), out_shape=[jax.Shap...  124 us
    sub x2, other arithmetic, adam(): plane - LEARN_RATE * (first * scale_one) / (jnp.sqrt(second * scale_two)...  2.7 us

profile of v4, /device:TPU:1, one launch (start us, length us, event | category | flops | bytes accessed | tf_op | source)
XLA Modules:
  0.0 131.8 jit_solution(10541033685419137127)
XLA Ops:
  0.6 0.7 convert_element_type.3
  2.0 0.0 copy-start.5
  2.0 0.6 copy-done.5
  2.6 0.6 maximum_bitcast_fusion.small
  3.2 123.9 %shard_map.205 = (f32[32,16,128]{2,1,0:T(8,128)}, f32[32,16,128]{2,1,0:T(8,128)}, f32[32,16,128]{2,1,0:T(8,128)}, f32[32,16,128]{2,1,0:T(8,128)}, f32[32,4,128]{...) custom-call(f32[16,128,128]{2,1,0:T(8,128)} %tgt.1, ...), custom_call_target="tpu_custom_call" | custom-call | tf_op jit(solution)/shard_map/pallas_call | solution.py:644
  127.1 0.0 copy-start.4
  127.1 0.0 copy-start.3
  127.1 1.7 %divide_subtract_fusion.1 = (f32[32,4,128]{2,1,0:T(4,128)}, f32[32,4,128]{2,1,0:T(4,128)}, f32[32,4,128]{2,1,0:T(4,128)}) fusion(f32[32,4,128]{2,1,0:T(4,128)} %get-tuple-element.29, f32[32,4,128]{2,1,0:T(4,128)} %get-tuple-element.31, f32[32,4,128]{2,1,0:T(4,128)} %get-tuple-element.30, f32[32,4,128]{2,1,0:T(4,128)} %get-tuple-element.32), kind=kLoop, calls=%fused_computation.10 | loop fusion | flops 196608 | bytes 458752 | tf_op jit(solution)/shard_map/sub | solution.py:92
  128.8 0.0 copy-done.4
  128.8 0.0 copy-start
  128.8 0.0 copy-start.1
  128.8 0.0 copy-start.2
  128.8 1.9 %fusion.4 = (f32[32,16,16]{0,2,1:T(8,128)}, f32[32,16,16]{0,2,1:T(8,128)}, f32[32,16,16]{0,2,1:T(8,128)}) fusion(f32[16,16,32]{2,1,0:T(8,128)} %get-tuple-element.27, f32[16,16,32]{2,1,0:T(8,128)} %get-tuple-element.28, f32[16,16,32]{2,1,0:T(8,128)S(1)} %copy-done.4, f32[16,16,32]{2,1,0:T(8,128)} %get-tuple-element.26), kind=kLoop, calls=%fused_computation.13 | loop fusion | flops 98304 | bytes 229376 | tf_op jit(solution)/shard_map/transpose | solution.py:724
  130.8 0.0 copy-done.3
  130.8 0.0 copy-done
  130.8 0.0 copy-done.1
  130.8 0.0 copy-done.2
  130.8 1.0 divide_subtract_fusion
  (1 shorter events, 0.0 us)
Async XLA Ops:
  2.0 0.7 copy-start.5
  127.1 1.8 %copy-start.4 = (f32[16,16,32]{2,1,0:T(8,128)S(1)}, f32[16,16,32]{2,1,0:T(8,128)}, u32[]{:S(2)}) copy-start(f32[16,16,32]{2,1,0:T(8,128)} %get-tuple-element.25) | copy-start | bytes 98308
  127.1 3.7 %copy-start.3 = (f32[32,16,128]{2,1,0:T(8,128)S(1)}, f32[32,16,128]{2,1,0:T(8,128)}, u32[]{:S(2)}) copy-start(f32[32,16,128]{2,1,0:T(8,128)} %get-tuple-element.23) | copy-start | bytes 786436
  128.8 1.9 %copy-start = (f32[32,16,128]{2,1,0:T(8,128)S(1)}, f32[32,16,128]{2,1,0:T(8,128)}, u32[]{:S(2)}) copy-start(f32[32,16,128]{2,1,0:T(8,128)} %get-tuple-element.21) | copy-start | bytes 786436
  128.8 2.0 %copy-start.1 = (f32[32,16,128]{2,1,0:T(8,128)S(1)}, f32[32,16,128]{2,1,0:T(8,128)}, u32[]{:S(2)}) copy-start(f32[32,16,128]{2,1,0:T(8,128)} %get-tuple-element.22) | copy-start | bytes 786436
  128.8 2.0 %copy-start.2 = (f32[32,16,128]{2,1,0:T(8,128)S(1)}, f32[32,16,128]{2,1,0:T(8,128)}, u32[]{:S(2)}) copy-start(f32[32,16,128]{2,1,0:T(8,128)} %get-tuple-element.24) | copy-start | bytes 786436

commit v5 on v4

--- a/solution.py
+++ b/solution.py
@@ -100,11 +100,11 @@
 def fit_kernel(
     nk,
     nj,
-    tgt, xy_in, xz_in, yz_in, mxy_in, mxz_in, myz_in, vxy_in, vxz_in, vyz_in, w_hidden, small,
+    tgt_in, xy_in, xz_in, yz_in, mxy_in, mxz_in, myz_in, vxy_in, vxz_in, vyz_in, w_hidden, small,
     xy_out, mxy_out, vxy_out, gxy_out, yz_out, myz_out, vyz_out, gyz_out, xz_out, mxz_out, vxz_out, gxz_out,
     xyp, mxy, vxy, mxz, vxz, gradxz, myz, vyz, xza, yza, gxy, gxz, gyz, sib, total, chain, saved, ypart, xparts,
     fbuf, dbuf, rbuf, row_out, row_in, col_out, col_in, w1, w2, wo, bh, wv,
-    load, store,
+    tgt, load, store,
     yz_recv, yz_send, relay_send, pass_send, xz_recv, xz_send, row_recv, row_send, col_recv, col_send,
     sib_recv, sib_send, chain_recv, chain_send, ypart_recv, ypart_send, xpart_recv, xpart_send,
 ):
@@ -166,13 +166,6 @@
         whole = src.at[pl.ds(first, count)]
         pltpu.make_async_copy(whole, whole, store.at[n]).wait()
 
-    loop(0, 4, lambda r: pltpu.make_async_copy(yz_in.at[:, r, :], yza.at[0, mine + r], load.at[1]).start())
-    load_rows(xy_in, xyp, 1, NX, 0)
-    load_rows(mxy_in, mxy, 0, NX, 2)
-    load_rows(vxy_in, vxy, 0, NX, 3)
-    load_rows(myz_in, myz, 0, 4, 4)
-    load_rows(vyz_in, vyz, 0, 4, 5)
-
     barrier = pltpu.get_barrier_semaphore()
 
     def greet(device):
@@ -187,6 +180,9 @@
     for device in (near(high, -toward, core), near(1 - high, -toward, core), border):
         greet(device)
     loop(1, nj, lambda r: greet((i, (j + r) % nj)))
+    loop(0, 4, lambda r: pltpu.make_async_copy(yz_in.at[:, r, :], yza.at[0, mine + r], load.at[1]).start())
+    load_rows(xy_in, xyp, 1, NX, 0)
+    pltpu.make_async_copy(tgt_in, tgt, load.at[6]).start()
 
     def gathered(src, n):
         return jnp.concatenate([src[:, 8 * n + z, :] for z in range(8)], axis=1)
@@ -597,6 +593,11 @@
     send_xz(0)
     loaded(xyp, 1, NX, 0)
     send_borders(0)
+    load_rows(mxy_in, mxy, 0, NX, 2)
+    load_rows(vxy_in, vxy, 0, NX, 3)
+    load_rows(myz_in, myz, 0, 4, 4)
+    load_rows(vyz_in, vyz, 0, 4, 5)
+    pltpu.make_async_copy(tgt_in, tgt, load.at[6]).wait()
     loop(0, STEPS, one_step)
     sent()
     xz_sent()
@@ -644,7 +645,7 @@
     outs = pl.pallas_call(
         functools.partial(fit_kernel, nk, nj),
         out_shape=[jax.ShapeDtypeStruct(shape, F32) for shape in shapes],
-        in_specs=[vm, far, vm, far, far, vm, far, far, vm, far, vm, vm],
+        in_specs=[far, far, vm, far, far, vm, far, far, vm, far, vm, vm],
         out_specs=[far] * 8 + [vm] * 4,
         scratch_shapes=[
             pltpu.VMEM((NX + 2, 32, 128), F32),
@@ -678,7 +679,8 @@
             pltpu.VMEM((16, 256), BF),
             pltpu.VMEM((32, 128), F32),
             pltpu.VMEM((32, 128), F32),
-            dma((6,)),
+            pltpu.VMEM((NX, 8 * nk, 128), F32),
+            dma((7,)),
             dma((8,)),
             dma((2, nz, 2, 3)),
             dma((7,)),

time: 132 us -> 131 us (level)
  no operation moved by 1% of the time
where the time goes in v5:
time: 131 us
  Pallas kernels  123 us (94%)
  other arithmetic  5.88 us (4%)
  between operations  1.36 us (1%)
    pallas_call x1, Pallas kernels, per_device(): pl.pallas_call(functools.partial(fit_kernel, nk, nj), out_shape=[jax.Shap...  123 us
    sub x2, other arithmetic, adam(): plane - LEARN_RATE * (first * scale_one) / (jnp.sqrt(second * scale_two)...  2.7 us

profile of v5, /device:TPU:1, one launch (start us, length us, event | category | flops | bytes accessed | tf_op | source)
XLA Modules:
  0.0 130.7 jit_solution(3049896501395309825)
XLA Ops:
  0.6 0.7 convert_element_type.3
  2.0 0.0 copy-start.5
  2.0 0.6 copy-done.5
  2.6 0.6 maximum_bitcast_fusion.small
  3.2 122.8 %shard_map.205 = (f32[32,16,128]{2,1,0:T(8,128)}, f32[32,16,128]{2,1,0:T(8,128)}, f32[32,16,128]{2,1,0:T(8,128)}, f32[32,16,128]{2,1,0:T(8,128)}, f32[32,4,128]{...) custom-call(f32[16,128,128]{2,1,0:T(8,128)} %tgt_in.1, ...), custom_call_target="tpu_custom_call" | custom-call | tf_op jit(solution)/shard_map/pallas_call | solution.py:645
  126.0 0.0 copy-start.4
  126.1 0.0 copy-start.3
  126.1 1.7 %divide_subtract_fusion.1 = (f32[32,4,128]{2,1,0:T(4,128)}, f32[32,4,128]{2,1,0:T(4,128)}, f32[32,4,128]{2,1,0:T(4,128)}) fusion(f32[32,4,128]{2,1,0:T(4,128)} %get-tuple-element.29, f32[32,4,128]{2,1,0:T(4,128)} %get-tuple-element.31, f32[32,4,128]{2,1,0:T(4,128)} %get-tuple-element.30, f32[32,4,128]{2,1,0:T(4,128)} %get-tuple-element.32), kind=kLoop, calls=%fused_computation.10 | loop fusion | flops 196608 | bytes 458752 | tf_op jit(solution)/shard_map/sub | solution.py:92
  127.8 0.0 copy-done.4
  127.8 0.0 copy-start
  127.8 0.0 copy-start.1
  127.8 0.0 copy-start.2
  127.8 1.9 %fusion.4 = (f32[32,16,16]{0,2,1:T(8,128)}, f32[32,16,16]{0,2,1:T(8,128)}, f32[32,16,16]{0,2,1:T(8,128)}) fusion(f32[16,16,32]{2,1,0:T(8,128)} %get-tuple-element.27, f32[16,16,32]{2,1,0:T(8,128)} %get-tuple-element.28, f32[16,16,32]{2,1,0:T(8,128)S(1)} %copy-done.4, f32[16,16,32]{2,1,0:T(8,128)} %get-tuple-element.26), kind=kLoop, calls=%fused_computation.13 | loop fusion | flops 98304 | bytes 229376 | tf_op jit(solution)/shard_map/transpose | solution.py:726
  129.7 0.0 copy-done.3
  129.7 0.0 copy-done
  129.8 0.0 copy-done.1
  129.8 0.0 copy-done.2
  129.8 1.0 divide_subtract_fusion
  (1 shorter events, 0.0 us)
Async XLA Ops:
  2.0 0.7 copy-start.5
  126.0 1.8 %copy-start.4 = (f32[16,16,32]{2,1,0:T(8,128)S(1)}, f32[16,16,32]{2,1,0:T(8,128)}, u32[]{:S(2)}) copy-start(f32[16,16,32]{2,1,0:T(8,128)} %get-tuple-element.25) | copy-start | bytes 98308
  126.1 3.7 %copy-start.3 = (f32[32,16,128]{2,1,0:T(8,128)S(1)}, f32[32,16,128]{2,1,0:T(8,128)}, u32[]{:S(2)}) copy-start(f32[32,16,128]{2,1,0:T(8,128)} %get-tuple-element.23) | copy-start | bytes 786436
  127.8 1.9 %copy-start = (f32[32,16,128]{2,1,0:T(8,128)S(1)}, f32[32,16,128]{2,1,0:T(8,128)}, u32[]{:S(2)}) copy-start(f32[32,16,128]{2,1,0:T(8,128)} %get-tuple-element.21) | copy-start | bytes 786436
  127.8 2.0 %copy-start.1 = (f32[32,16,128]{2,1,0:T(8,128)S(1)}, f32[32,16,128]{2,1,0:T(8,128)}, u32[]{:S(2)}) copy-start(f32[32,16,128]{2,1,0:T(8,128)} %get-tuple-element.22) | copy-start | bytes 786436
  127.8 2.0 %copy-start.2 = (f32[32,16,128]{2,1,0:T(8,128)S(1)}, f32[32,16,128]{2,1,0:T(8,128)}, u32[]{:S(2)}) copy-start(f32[32,16,128]{2,1,0:T(8,128)} %get-tuple-element.24) | copy-start | bytes 786436
